TPU v7x, 512 devices: a whole 4x8x8 slice. The times are simulated.
512 devices in a mesh: section: 2 (over x_lo), dp: 32 (over x_hi, z, core), tensor: 8 (over y).
Axes of the slice: x: 4 (x_hi: 2, x_lo: 2; x = x_hi * 2 + x_lo), y: 8, z: 8, core: 2. Of those that a mesh axis runs over, the one named last changes fastest.
Arguments:
- inputs: bfloat16 [2, 256, 8192], P(None, 'section', 'tensor'), may hold values from -6 to 6
- gain: float32 [8192], P('tensor'), may hold values from 0.1 to 1.9
- w_first: bfloat16 [8192, 16384], P('tensor', 'dp'), may hold values from -0.0625 to 0.0625
- w_second: bfloat16 [16384, 8192], P('dp', 'tensor'), may hold values from -0.046875 to 0.046875
- cotangent: bfloat16 [2, 256, 8192], P(None, ('section', 'dp'), 'tensor'), may hold values from -6 to 6
Outputs:
- outputs: bfloat16 [2, 256, 8192], P(None, ('section', 'dp'), 'tensor')
- input_grad: bfloat16 [2, 256, 8192], P(None, ('section', 'dp'), 'tensor')
- first_grad: bfloat16 [8192, 16384], P('tensor', 'dp')
- second_grad: bfloat16 [16384, 8192], P('dp', 'tensor')
- gain_grad: float32 [8192], P('tensor')
All inputs are finite; a program needn't handle non-finite values.
Results may differ from a plain program's by a relative error of at most 0.0067.
Values may be sent and summed in bfloat16 or wider, within the bound.
A program may use at most 64 MiB of HBM per device.

v0:
```python
import jax
import jax.numpy as jnp
from jax import lax
from jax.sharding import PartitionSpec as P

D = 8192


EPSILON = 1e-06


def per_device(inputs, gain, w_first, w_second, cotangent):
    batches = inputs.shape[0]
    group_tokens = inputs.shape[1]
    data_rows = group_tokens // lax.axis_size("dp")
    data_place = lax.axis_index("dp")
    values = inputs.astype(jnp.float32)
    first_sum = jnp.zeros(w_first.shape, jnp.float32)
    second_sum = jnp.zeros(w_second.shape, jnp.float32)
    gain_sum = jnp.zeros(gain.shape, jnp.float32)
    results = []
    gradients = []
    for index in range(batches):
        current = values[index]
        squares = lax.psum(jnp.sum(current * current, -1), "tensor")
        scale = lax.rsqrt(squares / D + EPSILON)[:, None]
        normed = (current * scale * gain).astype(jnp.bfloat16)
        partial_value = jnp.dot(normed, w_first, preferred_element_type=jnp.float32)
        pre_share = lax.psum_scatter(partial_value, "tensor", scatter_dimension=0, tiled=True)
        sig = jax.nn.sigmoid(pre_share)
        hidden = lax.all_gather(
            (pre_share * sig).astype(jnp.bfloat16), "tensor", axis=0, tiled=True
        )
        branch = lax.psum_scatter(
            jnp.dot(hidden, w_second, preferred_element_type=jnp.float32),
            "dp",
            scatter_dimension=0,
            tiled=True,
        )
        own_values = lax.dynamic_slice_in_dim(current, data_place * data_rows, data_rows, 0)
        own_scale = lax.dynamic_slice_in_dim(scale, data_place * data_rows, data_rows, 0)
        results.append((own_values + branch).astype(jnp.bfloat16))
        cot_all = lax.all_gather(cotangent[index], "dp", axis=0, tiled=True)
        second_sum = second_sum + jnp.einsum(
            "tk,tj->kj", hidden, cot_all, preferred_element_type=jnp.float32
        )
        grad_partial = jnp.einsum(
            "tj,kj->tk", cot_all, w_second, preferred_element_type=jnp.float32
        )
        slope = sig * (1.0 + pre_share * (1.0 - sig))
        own_grad = lax.psum_scatter(grad_partial, "tensor", scatter_dimension=0, tiled=True)
        pre_grad = lax.all_gather(
            (own_grad * slope).astype(jnp.bfloat16), "tensor", axis=0, tiled=True
        )
        first_sum = first_sum + jnp.einsum(
            "ti,tk->ik", normed, pre_grad, preferred_element_type=jnp.float32
        )
        normed_grad = lax.psum_scatter(
            jnp.einsum("tk,ik->ti", pre_grad, w_first, preferred_element_type=jnp.float32),
            "dp",
            scatter_dimension=0,
            tiled=True,
        )
        inner = lax.psum(jnp.sum(own_values * gain * normed_grad, -1), "tensor")[:, None]
        gradients.append(
            (
                cotangent[index].astype(jnp.float32)
                + own_scale * gain * normed_grad
                - own_values * own_scale**3 * inner / D
            ).astype(jnp.bfloat16)
        )
        gain_sum = gain_sum + jnp.sum(normed_grad * own_values * own_scale, 0)
    first_total, second_total = (
        lax.psum(first_sum.astype(jnp.bfloat16), "section").astype(jnp.float32),
        lax.psum(second_sum.astype(jnp.bfloat16), "section").astype(jnp.float32),
    )
    gain_total = lax.psum(gain_sum, ("section", "dp"))
    return (
        jnp.stack(results),
        jnp.stack(gradients),
        first_total.astype(jnp.bfloat16),
        second_total.astype(jnp.bfloat16),
        gain_total,
    )


def solution(mesh):
    in_specs = (
        P(None, "section", "tensor"),
        P("tensor"),
        P("tensor", "dp"),
        P("dp", "tensor"),
        P(None, ("section", "dp"), "tensor"),
    )
    out_specs = (
        P(None, ("section", "dp"), "tensor"),
        P(None, ("section", "dp"), "tensor"),
        P("tensor", "dp"),
        P("dp", "tensor"),
        P("tensor"),
    )
    return jax.shard_map(
        per_device, mesh=mesh, in_specs=in_specs, out_specs=out_specs, check_vma=False
    )
```

profile of v0, /device:TPU:1, one launch (start us, length us, event | category | flops | bytes accessed | tf_op | source)
XLA Modules:
  0.0 727.8 jit_solution(17213969287973774477)
XLA Ops:
  7.2 0.0 copy-start
  7.2 0.0 reduce-scatter.11.cloned.1.call-start
  7.2 0.8 fusion.51
  8.0 50.6 %all-gather.1 = bf16[1,128,1024]{2,0,1:T(2,128)(2,1)S(1)} all-gather(bf16[1,4,1024]{2,0,1:T(2,128)(2,1)S(1)} %copy.13), channel_id=3, replica_groups=mesh['section'=2,'dp'=32,'tensor'=8] {'dp'}, dimensions={1}, use_global_device_ids=true | all-gather | bytes 270336 | tf_op jit(solution)/shard_map/all_gather | solution.py:43
  58.7 0.8 copy-done.3
  59.5 0.0 copy-done
  59.5 1.2 fusion.7
  60.7 0.0 reduce-scatter.11.cloned.1.call-update
  60.7 0.0 reduce-scatter.7.cloned.1.call-start
  60.7 1.1 convert_element_type.49
  61.9 0.1 fusion.3
  62.0 14.1 %all-reduce.6 = (f32[128]{0:T(128)S(1)}, f32[128]{0:T(128)S(1)}) all-reduce(f32[128]{0:T(128)S(1)} %get-tuple-element.10, f32[128]{0:T(128)S(1)} %get-tuple-element.9), channel_id=1, replica_groups=mesh['section'=2,'dp'=32,'tensor'=8] {'tensor'}, use_global_device_ids=true, to_apply=%region_5.0 | all-reduce | flops 256 | bytes 2048 | tf_op jit(solution)/shard_map/psum | solution.py:25
  76.2 0.0 copy-done.1
  76.2 0.0 copy-done.9
  76.2 1.1 fusion.44
  77.2 0.0 reduce-scatter.7.cloned.1.call-update
  77.2 0.0 reduce-scatter.9.cloned.1.call-start
  77.3 41.3 %all-gather = bf16[1,128,1024]{2,0,1:T(2,128)(2,1)S(1)} all-gather(bf16[1,4,1024]{2,0,1:T(2,128)(2,1)S(1)} %copy.12), channel_id=2, replica_groups=mesh['section'=2,'dp'=32,'tensor'=8] {'dp'}, dimensions={1}, use_global_device_ids=true | all-gather | bytes 270336 | tf_op jit(solution)/shard_map/all_gather | solution.py:43
  118.7 0.8 copy-done.5
  119.5 1.2 fusion.11
  120.6 0.0 reduce-scatter.9.cloned.1.call-update
  120.7 0.0 reduce-scatter.5.cloned.1.call-start
  120.7 1.0 fusion.41
  121.8 0.0 reduce-scatter.5.cloned.1.call-update
  121.8 0.0 all-reduce.11.cloned.1.call-start
  121.8 0.0 reduce-scatter.11.cloned.1.call-done
  121.9 8.2 %reduce-scatter.7.cloned.1.call-done = f32[16,512]{1,0:T(8,128)} async-done(((f32[128,512]{1,0:T(8,128)}), f32[16,512]{1,0:T(8,128)}) %reduce-scatter.7.cloned.1.call-update) | async-done | bytes 32784 | tf_op jit(solution)/shard_map/reduce_scatter | solution.py:29
  130.0 1.4 multiply_convert_fusion
  131.4 18.4 %all_gather.19 = bf16[128,512]{1,0:T(8,128)(2,1)S(1)} all-gather(bf16[16,512]{1,0:T(8,128)(2,1)S(1)} %get-tuple-element.34), channel_id=1, replica_groups=mesh['section'=2,'dp'=32,'tensor'=8] {'tensor'}, dimensions={0}, use_global_device_ids=true | all-gather | bytes 147456 | tf_op jit(solution)/shard_map/all_gather | solution.py:31
  149.8 1.1 fusion.53
  150.9 19.5 %reduce-scatter.9.cloned.1.call-done = f32[16,512]{1,0:T(8,128)} async-done(((f32[128,512]{1,0:T(8,128)}), f32[16,512]{1,0:T(8,128)}) %reduce-scatter.9.cloned.1.call-update) | async-done | bytes 32784 | tf_op jit(solution)/shard_map/reduce_scatter | solution.py:51
  170.4 41.0 %reduce-scatter.5.cloned.1.call-done = f32[16,512]{1,0:T(8,128)} async-done(((f32[128,512]{1,0:T(8,128)}), f32[16,512]{1,0:T(8,128)}) %reduce-scatter.5.cloned.1.call-update) | async-done | bytes 32784 | tf_op jit(solution)/shard_map/reduce_scatter | solution.py:29
  211.3 0.8 multiply_convert_fusion.1
  212.1 18.2 %all_gather.18 = bf16[128,512]{1,0:T(8,128)(2,1)S(1)} all-gather(bf16[16,512]{1,0:T(8,128)(2,1)S(1)} %get-tuple-element.32), channel_id=1, replica_groups=mesh['section'=2,'dp'=32,'tensor'=8] {'tensor'}, dimensions={0}, use_global_device_ids=true | all-gather | bytes 147456 | tf_op jit(solution)/shard_map/all_gather | solution.py:31
  230.4 1.1 fusion.52
  231.5 18.5 %all_gather.23 = bf16[128,512]{1,0:T(8,128)(2,1)S(1)} all-gather(bf16[16,512]{1,0:T(8,128)(2,1)} %get-tuple-element.33), channel_id=1, replica_groups=mesh['section'=2,'dp'=32,'tensor'=8] {'tensor'}, dimensions={0}, use_global_device_ids=true | all-gather | bytes 147456 | tf_op jit(solution)/shard_map/all_gather | solution.py:52
  250.0 1.3 fusion.55
  251.2 18.4 %all_gather.21 = bf16[128,512]{1,0:T(8,128)(2,1)S(1)} all-gather(bf16[16,512]{1,0:T(8,128)(2,1)S(1)} %get-tuple-element.31), channel_id=1, replica_groups=mesh['section'=2,'dp'=32,'tensor'=8] {'tensor'}, dimensions={0}, use_global_device_ids=true | all-gather | bytes 147456 | tf_op jit(solution)/shard_map/all_gather | solution.py:52
  269.6 0.6 copy-done.6
  270.3 1.3 fusion.54
  271.6 0.0 all-reduce.11.cloned.1.call-update
  271.6 0.0 copy-start.4
  271.6 0.0 all-reduce.13.cloned.1.call-start
  271.7 1.6 fusion.9
  273.2 0.0 copy-done.7
  273.2 0.5 fusion.39
  273.8 0.0 copy-done.4
  273.8 1.4 add_convert_fusion
  275.2 1.5 add_convert_fusion.1
  276.7 0.0 all-reduce.13.cloned.1.call-update
  276.7 1.3 dynamic-slice.10
  278.7 0.1 multiply_multiply_fusion.1
  278.7 0.1 multiply_multiply_fusion
  278.8 0.0 copy-done.2
  278.8 0.1 fusion.50
  278.9 294.8 %all-reduce.11.cloned.1.call-done = (f32[128,1024]{1,0:T(8,128)}, f32[128,1024]{1,0:T(8,128)}, f32[128,1024]{1,0:T(8,128)}, f32[128,1024]{1,0:T(8,128)}) async-done(((f32[128,1024]{1,0:T(8,128)}, f32[128,1024]{1,0:T(8,128)}, f32[128,1024]{1,0:T(8,128)}, f32[128,1024]{1,0:T(8,128)}), (f32[128,1024]{1,0:T(8,128)}, f32[128,1024]{1,0:T(8,128)}, f32[128,1024]{1,0:T(8,128)}, ...) | async-done | bytes 2097168
  573.7 1.0 fusion.34
  574.7 13.2 %all-reduce.5 = (f32[4]{0:T(128)S(1)}, f32[4]{0:T(128)S(1)}) all-reduce(f32[4]{0:T(128)S(1)} %get-tuple-element.39, f32[4]{0:T(128)S(1)} %get-tuple-element.8), channel_id=1, replica_groups=mesh['section'=2,'dp'=32,'tensor'=8] {'tensor'}, use_global_device_ids=true, to_apply=%region_15.0 | all-reduce | flops 8 | bytes 64 | tf_op jit(solution)/shard_map/psum | solution.py:64
  588.0 128.1 %psum.55 = f32[1024]{0:T(1024)} all-reduce(f32[1024]{0:T(1024)S(1)} %add.88), channel_id=1, replica_groups=mesh['section'=2,'dp'=32,'tensor'=8] {'section','dp'}, use_global_device_ids=true, to_apply=%region_20.0 | all-reduce | flops 1024 | bytes 8192 | tf_op jit(solution)/shard_map/psum | solution.py:77
  716.1 0.0 copy-done.10
  716.1 0.9 fusion.37
  717.0 0.6 pad_maximum_fusion
  717.6 2.4 copy.38
  720.0 1.0 copy.39
  (16 shorter events, 0.1 us)
Async XLA Ops:
  7.2 52.3 %copy-start = (bf16[512,1024]{1,0:T(8,128)(2,1)S(1)}, bf16[512,1024]{1,0:T(8,128)(2,1)}, u32[]{:S(2)}) copy-start(bf16[512,1024]{1,0:T(8,128)(2,1)} %param.8) | copy-start | bytes 3145732
  7.2 114.7 %reduce-scatter.11.cloned.1.call-start = ((), (), s32[]{:S(2)}) async-start(), calls=%async_computation.7 | async-start | bytes 294912 | tf_op jit(solution)/shard_map/reduce_scatter | solution.py:51
  58.7 0.8 copy-start.3
  59.5 16.7 %copy-start.1 = (bf16[1024,512]{1,0:T(8,128)(2,1)S(1)}, bf16[1024,512]{1,0:T(8,128)(2,1)}, u32[]{:S(2)}) copy-start(bf16[1024,512]{1,0:T(8,128)(2,1)} %param.7) | copy-start | bytes 3145732
  59.5 16.7 %copy-start.9 = (f32[1024]{0:T(1024)S(1)}, f32[1024]{0:T(1024)}, u32[]{:S(2)}) copy-start(f32[1024]{0:T(1024)} %param.6) | copy-start | bytes 12292
  60.7 69.3 %reduce-scatter.7.cloned.1.call-start = ((), (), s32[]{:S(2)}) async-start(), calls=%async_computation.5 | async-start | bytes 294912 | tf_op jit(solution)/shard_map/reduce_scatter | solution.py:29
  77.2 93.1 %reduce-scatter.9.cloned.1.call-start = ((), (), s32[]{:S(2)}) async-start(), calls=%async_computation.6 | async-start | bytes 294912 | tf_op jit(solution)/shard_map/reduce_scatter | solution.py:51
  118.7 0.8 copy-start.5
  120.7 90.7 %reduce-scatter.5.cloned.1.call-start = ((), (), s32[]{:S(2)}) async-start(), calls=%async_computation.4 | async-start | bytes 294912 | tf_op jit(solution)/shard_map/reduce_scatter | solution.py:29
  121.8 451.9 %all-reduce.11.cloned.1.call-start = ((), (), s32[]{:S(2)}) async-start(), calls=%async_computation.8 | async-start | bytes 4194304
  269.6 0.7 copy-start.6
  271.6 1.7 copy-start.7
  271.6 2.2 copy-start.4
  271.6 446.0 %all-reduce.13.cloned.1.call-start = ((), (), s32[]{:S(2)}) async-start(), calls=%async_computation.9 | async-start | bytes 4194304 | tf_op jit(solution)/shard_map/psum | solution.py:74
  275.2 3.6 copy-start.2
  276.7 439.4 %copy-start.10 = (bf16[2,4,1024]{2,1,0:T(4,128)(2,1)S(1)}, bf16[2,4,1024]{2,1,0:T(4,128)(2,1)}, u32[]{:S(2)}) copy-start(bf16[2,4,1024]{2,1,0:T(4,128)(2,1)} %param.9) | copy-start | bytes 49156
  717.6 2.4 copy-start.8
Sparse Core Ops, SparseCore 0:
  60.8 27.5 reduce-scatter.10
  91.5 38.5 reduce-scatter.6
  132.8 37.5 reduce-scatter.8
  173.2 38.0 reduce-scatter.4
  271.7 301.9 all-reduce.10
  577.3 78.8 all-reduce.12
where the time goes:
time: 734 us; the launch traced here: 728 us
  waiting for transfers between devices  364 us (50%)
  blocking collectives  321 us (44%)
  between operations  14.9 us (2%)
  matrix products  14.3 us (2%)
  local copies, waits for them, and re-layouts  7.8 us (1%)
    unnamed x7, waiting for transfers between devices  295 us
    psum x1, blocking collectives, per_device(): gain_total = lax.psum(gain_sum, ('section', 'dp'))  128 us
    all_gather x2, blocking collectives, per_device(): cot_all = lax.all_gather(cotangent[index], 'dp', axis=0, tiled=True)  92 us
    reduce_scatter x2, waiting for transfers between devices, per_device(): lax.psum_scatter(partial_value, 'tensor', scatter_dimension=0, tiled=True)  49.1 us
    all_gather x2, blocking collectives, per_device(): lax.all_gather((own_grad * slope).astype(jnp.bfloat16), 'tensor', axis=0,...  36.9 us
    all_gather x2, blocking collectives, per_device(): lax.all_gather((pre_share * sig).astype(jnp.bfloat16), 'tensor', axis=0,...  36.6 us
    reduce_scatter x2, waiting for transfers between devices, per_device(): lax.psum_scatter(grad_partial, 'tensor', scatter_dimension=0, tiled=True)  19.5 us
  transfers between devices with their start and end apart: 6, of which 4 were waited for; matrix products, arithmetic and copies ran while one was open for 2% of the time, Pallas kernels for 0%

commit v1 on v0

v1 whole, which is shorter than its diff:
```python
import jax
import jax.numpy as jnp
from jax import lax
from jax.experimental import pallas as pl
from jax.experimental.pallas import tpu as pltpu
from jax.sharding import PartitionSpec as P

MESH = pl.DeviceIdType.MESH
F32 = jnp.float32
BF16 = jnp.bfloat16
D = 8192
EPSILON = 1e-06
N = 8
HID = 512
FEAT = 1024
EXT = HID + 128
WIDE = FEAT + 128
NT = (((1,), (1,)), ((), ()))
TN = (((0,), (0,)), ((), ()))


class Phase:
    count = 0

    def __init__(self, make, first, last, sems):
        self.make, self.first, self.last, self.sems = make, first, last, sems
        self.base = sems["used"]
        sems["used"] += last - first

    def copy(self, k):
        src, dst, device = self.make(k)
        place = self.base + k - self.first
        return pltpu.make_async_remote_copy(
            src_ref=src,
            dst_ref=dst,
            send_sem=self.sems["send"].at[place],
            recv_sem=self.sems["recv"].at[place],
            device_id=device,
            device_id_type=MESH,
        )

    def _each(self, what):
        if self.last - self.first == 1:
            what(self.copy(self.first))
            return

        def body(k, carry):
            what(self.copy(k))
            return carry

        lax.fori_loop(self.first, self.last, body, 0)

    def start(self):
        self.sems["phases"].append(self)
        self._each(lambda c: c.start())

    def arrived(self):
        self._each(lambda c: c.wait_recv())

    def sent(self):
        self._each(lambda c: c.wait_send())


COPIES = 160


def kernel(
    x_hbm, gain_ref, w1_hbm, w2_hbm, cot_ref,
    out_ref, ing_ref, first_hbm, second_hbm, gg_ref,
    x_in, w1, w2, xp, u, u_o, cg, cg_o,
    s_a, r_a, s_sq, r_sq, s_c, r_c, hid, hid_o, q, q_o, p_own, slope, scl,
    branch, r_fs, s_fz, r_fz, s_fx, r_fx,
    big, r_gs, s_gz, r_gz, s_gx, r_gx,
    gsum, g_sib, g_s2, g_lo, g_s4, g_z, g_s8, g_xh,
    first_out, second_out,
    send_sems, recv_sems, local_sems,
):
    s = lax.axis_index("section")
    d = lax.axis_index("dp")
    t = lax.axis_index("tensor")
    xh = d // 16
    z = lax.rem(d // 2, N)
    c = lax.rem(d, 2)

    def y_peer(k):
        return {"section": s, "dp": d, "tensor": lax.rem(t + k, N)}

    def z_place(k):
        return lax.rem(z + k, N)

    def z_peer(k):
        return {"section": s, "dp": xh * 16 + z_place(k) * 2 + c, "tensor": t}

    xh_peer = {"section": s, "dp": lax.rem(d + 16, 32), "tensor": t}
    sib_peer = {"section": s, "dp": d + 1 - 2 * c, "tensor": t}
    lo_peer = {"section": 1 - s, "dp": d, "tensor": t}

    sems = {"used": 0, "send": send_sems, "recv": recv_sems, "phases": []}

    load_x = pltpu.make_async_copy(x_hbm, x_in, local_sems.at[0])
    load_w1 = pltpu.make_async_copy(w1_hbm, w1, local_sems.at[1])
    load_w2 = pltpu.make_async_copy(w2_hbm, w2, local_sems.at[2])
    load_x.start()
    load_w1.start()
    load_w2.start()

    barrier = pltpu.get_barrier_semaphore()

    def greet(k, carry):
        pl.semaphore_signal(barrier, inc=1, device_id=y_peer(k), device_id_type=MESH)
        pl.semaphore_signal(barrier, inc=1, device_id=z_peer(k), device_id_type=MESH)
        return carry

    lax.fori_loop(1, N, greet, 0)
    for peer in (xh_peer, sib_peer, lo_peer):
        pl.semaphore_signal(barrier, inc=1, device_id=peer, device_id_type=MESH)

    def y_rows(k):
        return pl.ds(pl.multiple_of(16 * lax.rem(t + k, N), 16), 16)

    my_rows = y_rows(0)
    mine = 16 + c * 8 + z
    other = c * 8 + z

    cot_own = jnp.concatenate([cot_ref[0].astype(F32), cot_ref[1].astype(F32)], axis=0)
    cg[mine] = cot_own.astype(BF16)

    row = lax.broadcasted_iota(jnp.int32, (256, 256), 0)
    col = lax.broadcasted_iota(jnp.int32, (256, 256), 1)
    half = row // 128
    x_half = jnp.where(half == 1, xh, 1 - xh)
    owner = x_half * 16 + (lax.rem(row, 64) // 8) * 2 + lax.rem(row, 128) // 64
    token = (lax.rem(row, 8) // 4) * 128 + owner * 4 + lax.rem(row, 4)
    perm = jnp.where(col == token, 1.0, 0.0).astype(BF16)
    load_x.wait()
    x_flat = x_in[...].reshape(256, FEAT)
    xs = jnp.dot(perm, x_flat, preferred_element_type=F32)
    xp[...] = xs
    gain = gain_ref[...]
    u[...] = (xs * gain).astype(BF16).reshape(2, 128, FEAT)

    ones = jnp.ones((8, FEAT), BF16)
    squares = []
    for h in range(2):
        rows = xp[h * 128 : (h + 1) * 128, :]
        sq = rows * rows
        hi = sq.astype(BF16)
        lo = (sq - hi.astype(F32)).astype(BF16)
        squares.append(
            lax.dot_general(ones, hi, NT, preferred_element_type=F32)
            + lax.dot_general(ones, lo, NT, preferred_element_type=F32)
        )
    place = lax.broadcasted_iota(jnp.int32, (8, 128), 0)
    s_sq[...] = jnp.where(place == 0, squares[0], squares[1])

    pl.semaphore_wait(barrier, 2 * (N - 1) + 3)

    to_xh = Phase(lambda k: (cg.at[mine], cg.at[other], xh_peer), 0, 1, sems)
    to_xh.start()
    to_z = Phase(lambda k: (cg.at[mine], cg.at[mine], z_peer(k)), 1, N, sems)
    to_z.start()
    sq_y = Phase(lambda k: (s_sq, r_sq.at[k], y_peer(k)), 1, N, sems)
    sq_y.start()

    load_w1.wait()
    s_a[...] = (
        jnp.dot(u[...].reshape(256, FEAT), w1[...], preferred_element_type=F32)
        .astype(BF16)
        .reshape(2, 128, HID)
    )
    a_y = Phase(lambda k: (s_a.at[:, y_rows(k)], r_a.at[k], y_peer(k)), 1, N, sems)
    a_y.start()

    to_xh.arrived()
    to_z2 = Phase(lambda k: (cg.at[other], cg.at[other], z_peer(k)), 1, N, sems)
    to_z2.start()
    core_rows = pl.ds(pl.multiple_of(64 * c, 64), 64)
    u_lo = Phase(lambda k: (u.at[:, core_rows], u_o.at[:, core_rows], lo_peer), 0, 1, sems)
    u_lo.start()

    def pieces(h):
        return pl.ds(h * 16 + c * 8, 8)

    def gathered(h):
        return Phase(lambda k: (cg.at[pieces(h)], cg.at[pieces(h)], sib_peer), 0, 1, sems)

    def crossed(h):
        return Phase(lambda k: (cg.at[pieces(h)], cg_o.at[pieces(h)], lo_peer), 0, 1, sems)

    load_w2.wait()
    to_z.arrived()
    cot_sib1 = gathered(1)
    cot_sib1.start()
    to_z2.arrived()
    cot_sib0 = gathered(0)
    cot_sib0.start()

    def rows_of(pieces_ref, h):
        return pieces_ref[h * 16 : (h + 1) * 16].astype(F32).reshape(128, FEAT).astype(BF16)

    c_y = [
        Phase(lambda k, h=h: (s_c.at[h, y_rows(k)], r_c.at[k, h], y_peer(k)), 1, N, sems)
        for h in range(2)
    ]
    for h, arrived in ((1, cot_sib1), (0, cot_sib0)):
        arrived.arrived()
        s_c[h] = lax.dot_general(
            rows_of(cg, h), w2[...], NT, preferred_element_type=F32
        ).astype(BF16)
        c_y[h].start()
    cot_lo = [crossed(0), crossed(1)]
    cot_lo[0].start()
    cot_lo[1].start()

    sq_y.arrived()
    a_y.arrived()
    total_sq = s_sq[...]
    for k in range(1, N):
        total_sq = total_sq + r_sq[k]
    lane = lax.broadcasted_iota(jnp.int32, (16, 128), 1)
    spot = lax.broadcasted_iota(jnp.int32, (16, 128), 0) + 16 * t
    for h in range(2):
        picked = jnp.where(lane == spot, jnp.broadcast_to(total_sq[h : h + 1, :], (16, 128)), 0.0)
        scale = lax.rsqrt(jnp.sum(picked, axis=1, keepdims=True) / D + EPSILON)
        sums = s_a[h, my_rows].astype(F32)
        for k in range(1, N):
            sums = sums + r_a[k, h].astype(F32)
        pre = sums * scale
        sig = jax.nn.sigmoid(pre)
        hid[h, my_rows] = (pre * sig).astype(BF16)
        p_own[h] = sums
        slope[h] = sig * (1.0 + pre * (1.0 - sig))
        scl[h] = jnp.broadcast_to(scale, (16, 128))
    b_y = Phase(lambda k: (hid.at[:, my_rows], hid.at[:, my_rows], y_peer(k)), 1, N, sems)
    b_y.start()

    d_y = [
        Phase(lambda k, h=h: (q.at[h, my_rows], q.at[h, my_rows], y_peer(k)), 1, N, sems)
        for h in range(2)
    ]
    for h in (1, 0):
        c_y[h].arrived()
        sums = s_c[h, my_rows].astype(F32)
        for k in range(1, N):
            sums = sums + r_c[k, h].astype(F32)
        scale = scl[h][:, :1]
        own = sums * slope[h] * scale
        q[h, my_rows, 0:HID] = own.astype(BF16)
        terms = own * p_own[h]
        lanes = terms[:, 0:128] + terms[:, 128:256] + terms[:, 256:384] + terms[:, 384:512]
        q[h, my_rows, HID:EXT] = (lanes * (scale * scale / D)).astype(BF16)
        d_y[h].start()

    b_y.arrived()
    hid_lo = Phase(lambda k: (hid, hid_o, lo_peer), 0, 1, sems)
    hid_lo.start()
    branch[...] = jnp.dot(
        hid[...].reshape(256, HID), w2[...], preferred_element_type=F32
    ).reshape(2, 128, FEAT)
    sib_rows = pl.ds(pl.multiple_of(64 - 64 * c, 64), 64)
    f_sib = Phase(lambda k: (branch.at[:, sib_rows], r_fs, sib_peer), 0, 1, sems)
    f_sib.start()

    u_lo.arrived()
    u_sib = Phase(lambda k: (u_o.at[:, core_rows], u_o.at[:, core_rows], sib_peer), 0, 1, sems)
    u_sib.start()

    f_sib.arrived()
    for h in range(2):
        both = branch[h, core_rows] + r_fs[h]
        s_fz[h] = both.reshape(N, 8, FEAT).astype(BF16)
    f_z = Phase(
        lambda k: (s_fz.at[:, z_place(k)], r_fz.at[k], z_peer(k)), 1, N, sems
    )
    f_z.start()

    g_sibs = [
        Phase(lambda k, h=h: (big.at[h, sib_rows], r_gs.at[h], sib_peer), 0, 1, sems)
        for h in range(2)
    ]
    g_zs = [
        Phase(lambda k, h=h: (s_gz.at[h, z_place(k)], r_gz.at[h, k], z_peer(k)), 1, N, sems)
        for h in range(2)
    ]
    q_lo = [
        Phase(lambda k, h=h: (q.at[h], q_o.at[h], lo_peer), 0, 1, sems)
        for h in range(2)
    ]
    gain_part = jnp.zeros((1, FEAT), F32)
    for h in range(2):
        d_y[h].arrived()
        part = lax.dot_general(q[h, :, 0:HID], w1[...], NT, preferred_element_type=F32)
        big[h, :, 0:FEAT] = part
        big[h, :, FEAT:WIDE] = q[h, :, HID:EXT].astype(F32)
        g_sibs[h].start()
        q_lo[h].start()
        gain_part = gain_part + jnp.sum(
            part * xp[h * 128 : (h + 1) * 128, :], axis=0, keepdims=True
        )
        g_sibs[h].arrived()
        both = big[h, core_rows] + r_gs[h]
        s_gz[h] = both.reshape(N, 8, WIDE).astype(BF16)
        g_zs[h].start()

    gsum[...] = gain_part
    gg_sib = Phase(lambda k: (gsum, g_sib, sib_peer), 0, 1, sems)
    gg_sib.start()

    cot_sibo = [
        Phase(lambda k, h=h: (cg_o.at[pieces(h)], cg_o.at[pieces(h)], sib_peer), 0, 1, sems)
        for h in range(2)
    ]
    for h in range(2):
        cot_lo[h].arrived()
        cot_sibo[h].start()
    gg_sib.arrived()
    g_s2[...] = gsum[...] + g_sib[...]
    gg_lo = Phase(lambda k: (g_s2, g_lo, lo_peer), 0, 1, sems)
    gg_lo.start()

    hid_lo.arrived()
    for h in range(2):
        cot_sibo[h].arrived()
    second = jnp.zeros((HID, FEAT), F32)
    hid_all = jnp.concatenate(
        [hid[...].reshape(256, HID), hid_o[...].reshape(256, HID)], axis=0
    )
    cot_all = jnp.concatenate(
        [rows_of(cg, 0), rows_of(cg, 1), rows_of(cg_o, 0), rows_of(cg_o, 1)], axis=0
    )
    second_out[...] = lax.dot_general(
        hid_all, cot_all, TN, preferred_element_type=F32
    ).astype(BF16)
    save_second = pltpu.make_async_copy(second_out, second_hbm, local_sems.at[3])
    save_second.start()

    gg_lo.arrived()
    g_s4[...] = g_s2[...] + g_lo[...]
    gg_z = Phase(lambda k: (g_s4, g_z.at[k], z_peer(k)), 1, N, sems)
    gg_z.start()

    f_z.arrived()

    def z_total(sent, received, h):
        total = sent[h, z].astype(F32)
        for k in range(1, N):
            total = total + received(k)
        return total

    s_fx[...] = z_total(s_fz, lambda k: r_fz[k, 0].astype(F32), 0)
    f_xh = Phase(lambda k: (s_fx, r_fx, xh_peer), 0, 1, sems)
    f_xh.start()
    own_branch = z_total(s_fz, lambda k: r_fz[k, 1].astype(F32), 1)

    g_zs[0].arrived()
    s_gx[...] = z_total(s_gz, lambda k: r_gz[0, k].astype(F32), 0)
    g_xhp = Phase(lambda k: (s_gx, r_gx, xh_peer), 0, 1, sems)
    g_xhp.start()

    u_sib.arrived()
    for h in range(2):
        q_lo[h].arrived()
    u_all = jnp.concatenate([u[...].reshape(256, FEAT), u_o[...].reshape(256, FEAT)], axis=0)
    q_all = jnp.concatenate(
        [q[0, :, 0:HID], q[1, :, 0:HID], q_o[0, :, 0:HID], q_o[1, :, 0:HID]], axis=0
    )
    first_out[...] = lax.dot_general(u_all, q_all, TN, preferred_element_type=F32).astype(BF16)
    save_first = pltpu.make_async_copy(first_out, first_hbm, local_sems.at[4])
    save_first.start()

    gg_z.arrived()
    gain_total = g_s4[...]
    for k in range(1, N):
        gain_total = gain_total + g_z[k]
    g_s8[...] = gain_total
    gg_xh = Phase(lambda k: (g_s8, g_xh, xh_peer), 0, 1, sems)
    gg_xh.start()

    x_own = xp[pl.ds(pl.multiple_of(mine * 8, 8), 8), :]
    f_xh.arrived()
    outputs = x_own + own_branch + r_fx[...]
    out_ref[0] = outputs[0:4].astype(BF16)
    out_ref[1] = outputs[4:8].astype(BF16)

    g_zs[1].arrived()
    normed_grad = z_total(s_gz, lambda k: r_gz[1, k].astype(F32), 1)
    g_xhp.arrived()
    normed_grad = normed_grad + r_gx[...]
    inner = jnp.sum(normed_grad[:, FEAT:WIDE], axis=1, keepdims=True)
    grads = cg[mine].astype(F32) + gain * normed_grad[:, 0:FEAT] - x_own * inner
    ing_ref[0] = grads[0:4].astype(BF16)
    ing_ref[1] = grads[4:8].astype(BF16)

    gg_xh.arrived()
    gg_ref[...] = g_s8[...] + g_xh[...]

    for phase in sems["phases"]:
        phase.sent()
    save_second.wait()
    save_first.wait()


def per_device(inputs, gain, w_first, w_second, cotangent):
    vmem = pl.BlockSpec(memory_space=pltpu.VMEM)
    hbm = pl.BlockSpec(memory_space=pl.ANY)
    shapes = [
        ((2, 128, FEAT), BF16),
        ((FEAT, HID), BF16),
        ((HID, FEAT), BF16),
        ((256, FEAT), F32),
        ((2, 128, FEAT), BF16),
        ((2, 128, FEAT), BF16),
        ((32, 8, FEAT), BF16),
        ((32, 8, FEAT), BF16),
        ((2, 128, HID), BF16),
        ((N, 2, 16, HID), BF16),
        ((8, 128), F32),
        ((N, 8, 128), F32),
        ((2, 128, HID), BF16),
        ((N, 2, 16, HID), BF16),
        ((2, 128, HID), BF16),
        ((2, 128, HID), BF16),
        ((2, 128, EXT), BF16),
        ((2, 128, EXT), BF16),
        ((2, 16, HID), F32),
        ((2, 16, HID), F32),
        ((2, 16, 128), F32),
        ((2, 128, FEAT), F32),
        ((2, 64, FEAT), F32),
        ((2, N, 8, FEAT), BF16),
        ((N, 2, 8, FEAT), BF16),
        ((8, FEAT), F32),
        ((8, FEAT), F32),
        ((2, 128, WIDE), F32),
        ((2, 64, WIDE), F32),
        ((2, N, 8, WIDE), BF16),
        ((2, N, 8, WIDE), BF16),
        ((8, WIDE), F32),
        ((8, WIDE), F32),
        ((1, FEAT), F32),
        ((1, FEAT), F32),
        ((1, FEAT), F32),
        ((1, FEAT), F32),
        ((1, FEAT), F32),
        ((N, 1, FEAT), F32),
        ((1, FEAT), F32),
        ((1, FEAT), F32),
        ((FEAT, HID), BF16),
        ((HID, FEAT), BF16),
    ]
    outputs, input_grad, first_grad, second_grad, gain_grad = pl.pallas_call(
        kernel,
        out_shape=(
            jax.ShapeDtypeStruct(cotangent.shape, BF16),
            jax.ShapeDtypeStruct(cotangent.shape, BF16),
            jax.ShapeDtypeStruct(w_first.shape, BF16),
            jax.ShapeDtypeStruct(w_second.shape, BF16),
            jax.ShapeDtypeStruct((1, FEAT), F32),
        ),
        in_specs=[hbm, vmem, hbm, hbm, vmem],
        out_specs=(vmem, vmem, hbm, hbm, vmem),
        scratch_shapes=[pltpu.VMEM(shape, dtype) for shape, dtype in shapes]
        + [
            pltpu.SemaphoreType.DMA((COPIES,)),
            pltpu.SemaphoreType.DMA((COPIES,)),
            pltpu.SemaphoreType.DMA((5,)),
        ],
        compiler_params=pltpu.CompilerParams(
            collective_id=0, has_side_effects=True, vmem_limit_bytes=48 * 1024 * 1024
        ),
    )(inputs, gain.reshape(1, FEAT), w_first, w_second, cotangent)
    return outputs, input_grad, first_grad, second_grad, gain_grad.reshape(FEAT)


def solution(mesh):
    in_specs = (
        P(None, "section", "tensor"),
        P("tensor"),
        P("tensor", "dp"),
        P("dp", "tensor"),
        P(None, ("section", "dp"), "tensor"),
    )
    out_specs = (
        P(None, ("section", "dp"), "tensor"),
        P(None, ("section", "dp"), "tensor"),
        P("tensor", "dp"),
        P("dp", "tensor"),
        P("tensor"),
    )
    return jax.shard_map(
        per_device, mesh=mesh, in_specs=in_specs, out_specs=out_specs, check_vma=False
    )
```

time: 734 us -> 74.7 us (0.10)
  waiting for transfers between devices: 364 us -> 0 us
  blocking collectives: 321 us -> 0 us
  Pallas kernels: 0 us -> 64.7 us
  matrix products: 14.3 us -> 0 us
  between operations: 14.9 us -> 0.66 us
    unnamed x7 -> x0, waiting for transfers between devices: 295 us -> none
    all_gather x6 -> x0, blocking collectives: 165 us -> none  [the longest x2 92 us: per_device(): cot_all = lax.all_gather(cotangent[index], 'dp', axis=0, tiled=True)]
    psum x3 -> x0, blocking collectives: 155 us -> none  [the longest x1 128 us: per_device(): gain_total = lax.psum(gain_sum, ('section', 'dp'))]
    reduce_scatter x4 -> x0, waiting for transfers between devices: 68.6 us -> none  [the longest x2 49.1 us: per_device(): lax.psum_scatter(partial_value, 'tensor', scatter_dimension=0, tiled=True)]
    pallas_call x0 -> x1, Pallas kernels: none -> 64.7 us  [per_device(): pl.pallas_call(kernel, out_shape=(jax.ShapeDtypeStruct(cotangent.shape, B...]
    dot_general x12 -> x0, matrix products: 14.3 us -> none  [the longest x2 2.99 us: per_device(): jnp.einsum('tk,tj->kj', hidden, cot_all, preferred_element_type=jnp.float32)]
  transfers between devices with their start and end apart: 6 -> 0, of which waited for: 4 -> 0; matrix products, arithmetic and copies ran while one was open for 2% -> 0% of each run, Pallas kernels for 0% -> 0%
where the time goes in v1:
time: 74.7 us; the launch traced here: 74 us
  Pallas kernels  64.7 us (87%)
  local copies, waits for them, and re-layouts  8.63 us (12%)
    pallas_call x1, Pallas kernels, per_device(): pl.pallas_call(kernel, out_shape=(jax.ShapeDtypeStruct(cotangent.shape, B...  64.7 us
    unnamed x15, local copies, waits for them, and re-layouts  8.63 us

profile of v1, /device:TPU:1, one launch (start us, length us, event | category | flops | bytes accessed | tf_op | source)
XLA Modules:
  0.0 74.0 jit_solution(6033029764536051887)
XLA Ops:
  0.6 0.0 copy-start
  0.6 1.2 %copy-done = bf16[1024,512]{1,0:T(8,128)(2,1)S(1)} copy-done((bf16[1024,512]{1,0:T(8,128)(2,1)S(1)}, bf16[1024,512]{1,0:T(8,128)(2,1)}, u32[]{:S(2)}) %copy-start) | copy-done | bytes 1048600
  1.9 0.0 copy-start.1
  1.9 1.2 %copy-done.1 = bf16[512,1024]{1,0:T(8,128)(2,1)S(1)} copy-done((bf16[512,1024]{1,0:T(8,128)(2,1)S(1)}, bf16[512,1024]{1,0:T(8,128)(2,1)}, u32[]{:S(2)}) %copy-start.1) | copy-done | bytes 1048600
  3.1 0.0 copy-start.2
  3.1 1.0 %copy-done.2 = bf16[2,128,1024]{2,1,0:T(8,128)(2,1)S(1)} copy-done((bf16[2,128,1024]{2,1,0:T(8,128)(2,1)S(1)}, bf16[2,128,1024]{2,1,0:T(8,128)(2,1)}, u32[]{:S(2)}) %copy-start.2) | copy-done | bytes 524312
  4.1 0.0 copy-start.3
  4.1 0.7 copy-done.3
  4.8 0.0 copy-start.4
  4.8 0.7 copy-done.4
  5.5 64.7 %shard_map.92 = (bf16[2,4,1024]{2,1,0:T(4,128)(2,1)S(1)}, bf16[2,4,1024]{2,1,0:T(4,128)(2,1)S(1)}, bf16[1024,512]{1,0:T(8,128)(2,1)S(1)}, bf16[512,1024]{1,0:T(8,128)(2,1)S(1)}, f32[1,1024]{1,0:T(1,128)S(1)}) custom-call(bf16[2,128,1024]{2,1,0:T(8,128)(2,1)S(1)} %copy-done.2, f32[1,1024]{1,0:T(1,128)S(1)} %bitcast.2, bf16[1024,512]{1,0:T(8,128)(2,1)S(1)} %copy-done, ...), custom_call_target="tpu_custom_call" | custom-call | tf_op jit(solution)/shard_map/pallas_call | solution.py:451
  70.2 0.6 copy.15
  70.8 0.6 copy.16
  71.5 1.0 %copy.17 = bf16[1024,512]{1,0:T(8,128)(2,1)} copy(bf16[1024,512]{1,0:T(8,128)(2,1)S(1)} %get-tuple-element.22) | data formatting | bytes 2097152
  72.4 1.0 %copy.18 = bf16[512,1024]{1,0:T(8,128)(2,1)} copy(bf16[512,1024]{1,0:T(8,128)(2,1)S(1)} %get-tuple-element.23) | data formatting | bytes 2097152
  73.4 0.6 copy.19
Async XLA Ops:
  0.6 1.2 %copy-start = (bf16[1024,512]{1,0:T(8,128)(2,1)S(1)}, bf16[1024,512]{1,0:T(8,128)(2,1)}, u32[]{:S(2)}) copy-start(bf16[1024,512]{1,0:T(8,128)(2,1)} %w1_hbm.1) | copy-start | bytes 3145732
  1.9 1.2 %copy-start.1 = (bf16[512,1024]{1,0:T(8,128)(2,1)S(1)}, bf16[512,1024]{1,0:T(8,128)(2,1)}, u32[]{:S(2)}) copy-start(bf16[512,1024]{1,0:T(8,128)(2,1)} %w2_hbm.1) | copy-start | bytes 3145732
  3.1 1.0 %copy-start.2 = (bf16[2,128,1024]{2,1,0:T(8,128)(2,1)S(1)}, bf16[2,128,1024]{2,1,0:T(8,128)(2,1)}, u32[]{:S(2)}) copy-start(bf16[2,128,1024]{2,1,0:T(8,128)(2,1)} %x_hbm.1) | copy-start | bytes 1572868
  4.1 0.7 copy-start.3
  4.8 0.7 copy-start.4

commit v2 on v1

v2 whole, which is shorter than its diff:
```python
import jax
import jax.numpy as jnp
from jax import lax
from jax.experimental import pallas as pl
from jax.experimental.pallas import tpu as pltpu
from jax.sharding import PartitionSpec as P

MESH = pl.DeviceIdType.MESH
F32 = jnp.float32
BF16 = jnp.bfloat16
D = 8192
EPSILON = 1e-06
N = 8
HID = 512
FEAT = 1024
ROW = FEAT + 256
NT = (((1,), (1,)), ((), ()))
TN = (((0,), (0,)), ((), ()))


class Phase:
    def __init__(self, make, first, last, sems):
        self.make, self.first, self.last, self.sems = make, first, last, sems
        self.base = sems["used"]
        sems["used"] += last - first

    def copy(self, k):
        src, dst, device = self.make(k)
        place = self.base + k - self.first
        return pltpu.make_async_remote_copy(
            src_ref=src,
            dst_ref=dst,
            send_sem=self.sems["send"].at[place],
            recv_sem=self.sems["recv"].at[place],
            device_id=device,
            device_id_type=MESH,
        )

    def _each(self, what):
        if self.last - self.first == 1:
            what(self.copy(self.first))
            return

        def body(k, carry):
            what(self.copy(k))
            return carry

        lax.fori_loop(self.first, self.last, body, 0)

    def start(self):
        self.sems["phases"].append(self)
        self._each(lambda c: c.start())

    def arrived(self):
        self._each(lambda c: c.wait_recv())

    def sent(self):
        self._each(lambda c: c.wait_send())


COPIES = 160


def kernel(
    x_hbm, gain_hbm, w1_hbm, w2_hbm, cot_hbm,
    out_ref, ing_ref, first_out, second_out, gg_ref,
    x_in, gain_ref, w1, w2, cot_ref, xp, u, u_o, cg, cg_o,
    s_a, r_a, s_sq, r_sq, s_c, r_c, hid, hid_o, q, q_o, p_own, slope, scl,
    branch, r_fs, s_fz, r_fz, s_fx, r_fx,
    big, r_gs, s_gz, r_gz, s_gx, r_gx,
    e_s, e_r, gg_own, gg_r1, gg_chip, gg_rz, gg_line, gg_rx,
    send_sems, recv_sems, local_sems,
):
    s = lax.axis_index("section")
    d = lax.axis_index("dp")
    t = lax.axis_index("tensor")
    xh = d // 16
    z = lax.rem(d // 2, N)
    c = lax.rem(d, 2)

    def y_peer(k):
        return {"section": s, "dp": d, "tensor": lax.rem(t + k, N)}

    def z_place(k):
        return lax.rem(z + k, N)

    def z_peer(k):
        return {"section": s, "dp": xh * 16 + z_place(k) * 2 + c, "tensor": t}

    xh_peer = {"section": s, "dp": lax.rem(d + 16, 32), "tensor": t}
    sib_peer = {"section": s, "dp": d + 1 - 2 * c, "tensor": t}
    lo_peer = {"section": 1 - s, "dp": d, "tensor": t}
    far_peer = {"section": 1 - s, "dp": lax.rem(d + 16, 32), "tensor": t}

    sems = {"used": 0, "send": send_sems, "recv": recv_sems, "phases": []}

    load_cot = pltpu.make_async_copy(cot_hbm, cot_ref, local_sems.at[0])
    load_gain = pltpu.make_async_copy(gain_hbm, gain_ref, local_sems.at[1])
    load_x = pltpu.make_async_copy(x_hbm, x_in, local_sems.at[2])
    load_w1 = pltpu.make_async_copy(w1_hbm, w1, local_sems.at[3])
    load_w2 = pltpu.make_async_copy(w2_hbm, w2, local_sems.at[4])
    for load in (load_cot, load_gain, load_x, load_w1, load_w2):
        load.start()

    barrier = pltpu.get_barrier_semaphore()

    def greet(k, carry):
        pl.semaphore_signal(barrier, inc=1, device_id=y_peer(k), device_id_type=MESH)
        pl.semaphore_signal(barrier, inc=1, device_id=z_peer(k), device_id_type=MESH)
        return carry

    lax.fori_loop(1, N, greet, 0)
    for peer in (xh_peer, sib_peer, lo_peer, far_peer):
        pl.semaphore_signal(barrier, inc=1, device_id=peer, device_id_type=MESH)

    def y_rows(k):
        return pl.ds(pl.multiple_of(16 * lax.rem(t + k, N), 16), 16)

    my_rows = y_rows(0)
    mine = 16 + c * 8 + z
    other = c * 8 + z

    load_cot.wait()
    cot_own = jnp.concatenate([cot_ref[0].astype(F32), cot_ref[1].astype(F32)], axis=0)
    cg[mine] = cot_own.astype(BF16)

    pl.semaphore_wait(barrier, 2 * (N - 1) + 4)

    to_xh = Phase(lambda k: (cg.at[mine], cg.at[other], xh_peer), 0, 1, sems)
    to_xh.start()
    to_z = Phase(lambda k: (cg.at[mine], cg.at[mine], z_peer(k)), 1, N, sems)
    to_z.start()

    row = lax.broadcasted_iota(jnp.int32, (256, 256), 0)
    col = lax.broadcasted_iota(jnp.int32, (256, 256), 1)
    x_half = jnp.where(row // 128 == 1, xh, 1 - xh)
    owner = x_half * 16 + (lax.rem(row, 64) // 8) * 2 + lax.rem(row, 128) // 64
    token = (lax.rem(row, 8) // 4) * 128 + owner * 4 + lax.rem(row, 4)
    perm = jnp.where(col == token, 1.0, 0.0).astype(BF16)
    load_x.wait()
    x_flat = x_in[...].reshape(256, FEAT)
    xs = jnp.dot(perm, x_flat, preferred_element_type=F32)
    xp[...] = xs
    load_gain.wait()
    gain = gain_ref[...]
    u[...] = (xs * gain).astype(BF16).reshape(2, 128, FEAT)
    load_w1.wait()
    s_a[...] = (
        jnp.dot(u[...].reshape(256, FEAT), w1[...], preferred_element_type=F32)
        .astype(BF16)
        .reshape(2, 128, HID)
    )
    a_y = Phase(lambda k: (s_a.at[:, y_rows(k)], r_a.at[k], y_peer(k)), 1, N, sems)
    a_y.start()

    ones = jnp.ones((8, FEAT), BF16)
    squares = []
    for h in range(2):
        rows = xp[h * 128 : (h + 1) * 128, :]
        sq = rows * rows
        hi = sq.astype(BF16)
        lo = (sq - hi.astype(F32)).astype(BF16)
        squares.append(
            lax.dot_general(ones, hi, NT, preferred_element_type=F32)
            + lax.dot_general(ones, lo, NT, preferred_element_type=F32)
        )
    place = lax.broadcasted_iota(jnp.int32, (8, 128), 0)
    s_sq[...] = jnp.where(place == 0, squares[0], squares[1])
    sq_y = Phase(lambda k: (s_sq, r_sq.at[k], y_peer(k)), 1, N, sems)
    sq_y.start()

    to_xh.arrived()
    to_z2 = Phase(lambda k: (cg.at[other], cg.at[other], z_peer(k)), 1, N, sems)
    to_z2.start()
    core_rows = pl.ds(pl.multiple_of(64 * c, 64), 64)
    u_lo = Phase(lambda k: (u.at[:, core_rows], u_o.at[:, core_rows], lo_peer), 0, 1, sems)
    u_lo.start()

    def pieces(h):
        return pl.ds(h * 16 + c * 8, 8)

    def gathered(h):
        return Phase(lambda k: (cg.at[pieces(h)], cg.at[pieces(h)], sib_peer), 0, 1, sems)

    def crossed(h):
        return Phase(lambda k: (cg.at[pieces(h)], cg_o.at[pieces(h)], lo_peer), 0, 1, sems)

    def rows_of(pieces_ref, h):
        return pieces_ref[h * 16 : (h + 1) * 16].astype(F32).reshape(128, FEAT).astype(BF16)

    c_y = [
        Phase(lambda k, h=h: (s_c.at[h, y_rows(k)], r_c.at[k, h], y_peer(k)), 1, N, sems)
        for h in range(2)
    ]

    def send_c(h):
        s_c[h] = lax.dot_general(
            rows_of(cg, h), w2[...], NT, preferred_element_type=F32
        ).astype(BF16)
        c_y[h].start()

    load_w2.wait()
    to_z.arrived()
    cot_sib1 = gathered(1)
    cot_sib1.start()
    cot_sib1.arrived()
    send_c(1)
    cot_lo1 = crossed(1)
    cot_lo1.start()

    sq_y.arrived()
    total_sq = s_sq[...]
    for k in range(1, N):
        total_sq = total_sq + r_sq[k]
    lane = lax.broadcasted_iota(jnp.int32, (16, 128), 1)
    spot = lax.broadcasted_iota(jnp.int32, (16, 128), 0) + 16 * t
    a_y.arrived()
    for h in range(2):
        picked = jnp.where(lane == spot, jnp.broadcast_to(total_sq[h : h + 1, :], (16, 128)), 0.0)
        scale = lax.rsqrt(jnp.sum(picked, axis=1, keepdims=True) / D + EPSILON)
        sums = s_a[h, my_rows].astype(F32)
        for k in range(1, N):
            sums = sums + r_a[k, h].astype(F32)
        pre = sums * scale
        sig = jax.nn.sigmoid(pre)
        hid[h, my_rows] = (pre * sig).astype(BF16)
        p_own[h] = sums
        slope[h] = sig * (1.0 + pre * (1.0 - sig))
        scl[h] = jnp.broadcast_to(scale, (16, 128))

    b_near = Phase(
        lambda k: (hid.at[:, my_rows], hid.at[:, my_rows], y_peer(1 + 6 * k)), 0, 2, sems
    )
    b_near.start()

    to_z2.arrived()
    cot_sib0 = gathered(0)
    cot_sib0.start()
    cot_sib0.arrived()
    send_c(0)
    cot_lo0 = crossed(0)
    cot_lo0.start()

    b_near.arrived()
    left_rows, right_rows = y_rows(N - 1), y_rows(1)
    b_right = Phase(
        lambda k: (hid.at[:, left_rows], hid.at[:, left_rows], y_peer(k)), 1, 3, sems
    )
    b_left = Phase(
        lambda k: (hid.at[:, right_rows], hid.at[:, right_rows], y_peer(N - k)), 1, 3, sems
    )
    b_right3 = Phase(
        lambda k: (hid.at[0, left_rows], hid.at[0, left_rows], y_peer(3)), 0, 1, sems
    )
    b_left3 = Phase(
        lambda k: (hid.at[1, right_rows], hid.at[1, right_rows], y_peer(N - 3)), 0, 1, sems
    )
    b_rest = (b_right3, b_left3, b_right, b_left)
    for phase in b_rest:
        phase.start()

    d_y = [
        Phase(lambda k, h=h: (q.at[h, my_rows], q.at[h, my_rows], y_peer(k)), 1, N, sems)
        for h in range(2)
    ]
    for h in (1, 0):
        c_y[h].arrived()
        sums = s_c[h, my_rows].astype(F32)
        for k in range(1, N):
            sums = sums + r_c[k, h].astype(F32)
        scale = scl[h][:, :1]
        own = sums * slope[h] * scale
        q[h, my_rows] = own.astype(BF16)
        if h == 0:
            d_y[0].start()
            d_y[1].start()
        inner = jnp.sum(own * p_own[h], axis=1, keepdims=True) * (scale * scale / D)
        e_s[:, h * 128 : (h + 1) * 128] = jnp.sum(
            jnp.where(lane == spot, inner, 0.0), axis=0, keepdims=True
        )
    e_y = Phase(lambda k: (e_s, e_r.at[k], y_peer(k)), 1, N, sems)
    e_y.start()

    for phase in b_rest:
        phase.arrived()
    hid_lo = Phase(lambda k: (hid, hid_o, lo_peer), 0, 1, sems)
    hid_lo.start()
    branch[...] = jnp.dot(
        hid[...].reshape(256, HID), w2[...], preferred_element_type=F32
    ).reshape(2, 128, FEAT)
    sib_rows = pl.ds(pl.multiple_of(64 - 64 * c, 64), 64)
    f_sib = Phase(lambda k: (branch.at[:, sib_rows], r_fs, sib_peer), 0, 1, sems)
    f_sib.start()

    u_lo.arrived()
    u_sib = Phase(lambda k: (u_o.at[:, core_rows], u_o.at[:, core_rows], sib_peer), 0, 1, sems)
    u_sib.start()

    f_sib.arrived()
    for h in range(2):
        both = branch[h, core_rows] + r_fs[h]
        s_fz[h] = both.reshape(N, 8, FEAT).astype(BF16)
    f_z = Phase(
        lambda k: (s_fz.at[:, z_place(k)], r_fz.at[k], z_peer(k)), 1, N, sems
    )
    f_z.start()

    g_sibs = [
        Phase(lambda k, h=h: (big.at[h, sib_rows], r_gs.at[h], sib_peer), 0, 1, sems)
        for h in range(2)
    ]
    g_zs = [
        Phase(lambda k, h=h: (s_gz.at[h, z_place(k)], r_gz.at[h, k], z_peer(k)), 1, N, sems)
        for h in range(2)
    ]
    q_lo = [
        Phase(lambda k, h=h: (q.at[h], q_o.at[h], lo_peer), 0, 1, sems)
        for h in range(2)
    ]
    gain_part = jnp.zeros((1, FEAT), F32)
    for h in range(2):
        d_y[h].arrived()
        part = lax.dot_general(q[h], w1[...], NT, preferred_element_type=F32)
        big[h] = part
        g_sibs[h].start()
        q_lo[h].start()
        gain_part = gain_part + jnp.sum(
            part * xp[h * 128 : (h + 1) * 128, :], axis=0, keepdims=True
        )
        if h == 1:
            e_y.arrived()
            e_sum = e_s[...]
            for k in range(1, N):
                e_sum = e_sum + e_r[k]
            gg_own[:, 0:FEAT] = gain_part
            gg_own[:, FEAT:ROW] = e_sum
            gg_sib = Phase(lambda k: (gg_own, gg_r1, sib_peer), 0, 1, sems)
            gg_sib.start()
        g_sibs[h].arrived()
        both = big[h, core_rows] + r_gs[h]
        s_gz[h] = both.reshape(N, 8, FEAT).astype(BF16)
        g_zs[h].start()
    gg_sib.arrived()
    gg_chip[...] = gg_own[...] + gg_r1[...]
    gg_z = Phase(lambda k: (gg_chip, gg_rz.at[k], z_peer(k)), 1, N, sems)
    gg_z.start()

    cot_sibo = [
        Phase(lambda k, h=h: (cg_o.at[pieces(h)], cg_o.at[pieces(h)], sib_peer), 0, 1, sems)
        for h in range(2)
    ]
    cot_lo1.arrived()
    cot_sibo[1].start()
    cot_lo0.arrived()
    cot_sibo[0].start()
    hid_lo.arrived()
    for h in range(2):
        cot_sibo[h].arrived()
    hid_all = jnp.concatenate(
        [hid[...].reshape(256, HID), hid_o[...].reshape(256, HID)], axis=0
    )
    cot_all = jnp.concatenate(
        [rows_of(cg, 0), rows_of(cg, 1), rows_of(cg_o, 0), rows_of(cg_o, 1)], axis=0
    )
    second_out[...] = lax.dot_general(
        hid_all, cot_all, TN, preferred_element_type=F32
    ).astype(BF16)

    def z_total(sent, received, h):
        total = sent[h, z].astype(F32)
        for k in range(1, N):
            total = total + received(k)
        return total

    f_z.arrived()
    s_fx[...] = z_total(s_fz, lambda k: r_fz[k, 0].astype(F32), 0)
    f_xh = Phase(lambda k: (s_fx, r_fx, xh_peer), 0, 1, sems)
    f_xh.start()
    own_branch = z_total(s_fz, lambda k: r_fz[k, 1].astype(F32), 1)

    g_zs[0].arrived()
    s_gx[...] = z_total(s_gz, lambda k: r_gz[0, k].astype(F32), 0)
    g_xh = Phase(lambda k: (s_gx, r_gx, xh_peer), 0, 1, sems)
    g_xh.start()

    gg_z.arrived()
    gg_total = gg_chip[...]
    for k in range(1, N):
        gg_total = gg_total + gg_rz[k]
    gg_line[...] = gg_total
    gg_x = [
        Phase(lambda k, i=i, peer=peer: (gg_line, gg_rx.at[i], peer), 0, 1, sems)
        for i, peer in enumerate((xh_peer, lo_peer, far_peer))
    ]
    for phase in gg_x:
        phase.start()

    u_sib.arrived()
    for h in range(2):
        q_lo[h].arrived()
    u_all = jnp.concatenate([u[...].reshape(256, FEAT), u_o[...].reshape(256, FEAT)], axis=0)
    q_all = jnp.concatenate(
        [q[...].reshape(256, HID), q_o[...].reshape(256, HID)], axis=0
    )
    first_out[...] = lax.dot_general(u_all, q_all, TN, preferred_element_type=F32).astype(BF16)

    x_own = xp[pl.ds(pl.multiple_of(mine * 8, 8), 8), :]
    f_xh.arrived()
    outputs = x_own + own_branch + r_fx[...]
    out_ref[0] = outputs[0:4].astype(BF16)
    out_ref[1] = outputs[4:8].astype(BF16)

    g_zs[1].arrived()
    normed_grad = z_total(s_gz, lambda k: r_gz[1, k].astype(F32), 1)
    g_xh.arrived()
    normed_grad = normed_grad + r_gx[...]
    for phase in gg_x:
        phase.arrived()
    inner_row = gg_line[:, FEAT + 128 : ROW] + gg_rx[0][:, FEAT : FEAT + 128]
    own_lane = lax.broadcasted_iota(jnp.int32, (8, 128), 1)
    own_spot = lax.broadcasted_iota(jnp.int32, (8, 128), 0) + c * 64 + z * 8
    inner = jnp.sum(
        jnp.where(own_lane == own_spot, jnp.broadcast_to(inner_row, (8, 128)), 0.0),
        axis=1,
        keepdims=True,
    )
    grads = cg[mine].astype(F32) + gain * normed_grad - x_own * inner
    ing_ref[0] = grads[0:4].astype(BF16)
    ing_ref[1] = grads[4:8].astype(BF16)
    gg_ref[...] = (gg_line[:, 0:FEAT] + gg_rx[0][:, 0:FEAT]) + (
        gg_rx[1][:, 0:FEAT] + gg_rx[2][:, 0:FEAT]
    )

    for phase in sems["phases"]:
        phase.sent()


def save(*refs):
    sources, targets, sems = refs[:5], refs[5:10], refs[10]
    copies = [pltpu.make_async_copy(sources[i], targets[i], sems.at[i]) for i in range(5)]
    for copy in copies:
        copy.start()
    for copy in copies:
        copy.wait()


def per_device(inputs, gain, w_first, w_second, cotangent):
    vmem = pl.BlockSpec(memory_space=pltpu.VMEM)
    hbm = pl.BlockSpec(memory_space=pltpu.HBM)
    anywhere = pl.BlockSpec(memory_space=pl.ANY)
    shapes = [
        ((2, 128, FEAT), BF16),
        ((1, FEAT), F32),
        ((FEAT, HID), BF16),
        ((HID, FEAT), BF16),
        ((2, 4, FEAT), BF16),
        ((256, FEAT), F32),
        ((2, 128, FEAT), BF16),
        ((2, 128, FEAT), BF16),
        ((32, 8, FEAT), BF16),
        ((32, 8, FEAT), BF16),
        ((2, 128, HID), BF16),
        ((N, 2, 16, HID), BF16),
        ((8, 128), F32),
        ((N, 8, 128), F32),
        ((2, 128, HID), BF16),
        ((N, 2, 16, HID), BF16),
        ((2, 128, HID), BF16),
        ((2, 128, HID), BF16),
        ((2, 128, HID), BF16),
        ((2, 128, HID), BF16),
        ((2, 16, HID), F32),
        ((2, 16, HID), F32),
        ((2, 16, 128), F32),
        ((2, 128, FEAT), F32),
        ((2, 64, FEAT), F32),
        ((2, N, 8, FEAT), BF16),
        ((N, 2, 8, FEAT), BF16),
        ((8, FEAT), F32),
        ((8, FEAT), F32),
        ((2, 128, FEAT), F32),
        ((2, 64, FEAT), F32),
        ((2, N, 8, FEAT), BF16),
        ((2, N, 8, FEAT), BF16),
        ((8, FEAT), F32),
        ((8, FEAT), F32),
        ((1, 256), F32),
        ((N, 1, 256), F32),
        ((1, ROW), F32),
        ((1, ROW), F32),
        ((1, ROW), F32),
        ((N, 1, ROW), F32),
        ((1, ROW), F32),
        ((3, 1, ROW), F32),
    ]
    results = (
        jax.ShapeDtypeStruct(cotangent.shape, BF16),
        jax.ShapeDtypeStruct(cotangent.shape, BF16),
        jax.ShapeDtypeStruct(w_first.shape, BF16),
        jax.ShapeDtypeStruct(w_second.shape, BF16),
        jax.ShapeDtypeStruct((1, FEAT), F32),
    )
    made = pl.pallas_call(
        kernel,
        out_shape=results,
        in_specs=[hbm] * 5,
        out_specs=(vmem,) * 5,
        scratch_shapes=[pltpu.VMEM(shape, dtype) for shape, dtype in shapes]
        + [
            pltpu.SemaphoreType.DMA((COPIES,)),
            pltpu.SemaphoreType.DMA((COPIES,)),
            pltpu.SemaphoreType.DMA((5,)),
        ],
        compiler_params=pltpu.CompilerParams(
            collective_id=0, has_side_effects=True, vmem_limit_bytes=48 * 1024 * 1024
        ),
    )(
        *(
            pltpu.with_memory_space_constraint(array, pltpu.HBM)
            for array in (inputs, gain.reshape(1, FEAT), w_first, w_second, cotangent)
        )
    )
    outputs, input_grad, first_grad, second_grad, gain_grad = pl.pallas_call(
        save,
        out_shape=results,
        in_specs=[anywhere] * 5,
        out_specs=(hbm,) * 5,
        scratch_shapes=[pltpu.SemaphoreType.DMA((5,))],
    )(*made)
    return outputs, input_grad, first_grad, second_grad, gain_grad.reshape(FEAT)


def solution(mesh):
    in_specs = (
        P(None, "section", "tensor"),
        P("tensor"),
        P("tensor", "dp"),
        P("dp", "tensor"),
        P(None, ("section", "dp"), "tensor"),
    )
    out_specs = (
        P(None, ("section", "dp"), "tensor"),
        P(None, ("section", "dp"), "tensor"),
        P("tensor", "dp"),
        P("dp", "tensor"),
        P("tensor"),
    )
    return jax.shard_map(
        per_device, mesh=mesh, in_specs=in_specs, out_specs=out_specs, check_vma=False
    )
```

time: 74.7 us -> 132 us (1.77)
  Pallas kernels: 64.7 us -> 127 us
  local copies, waits for them, and re-layouts: 8.63 us -> 3.78 us
    pallas_call x1 -> x2, Pallas kernels: 64.7 us -> 127 us  [the longest x1 65.8 us: per_device(): pl.pallas_call(save, out_shape=results, in_specs=[anywhere] * 5, out_spec...]
    unnamed x15 -> x10, local copies, waits for them, and re-layouts: 8.63 us -> 3.78 us
where the time goes in v2:
time: 132 us
  Pallas kernels  127 us (96%)
  local copies, waits for them, and re-layouts  3.78 us (3%)
    pallas_call x1, Pallas kernels, per_device(): pl.pallas_call(save, out_shape=results, in_specs=[anywhere] * 5, out_spec...  65.8 us
    pallas_call x1, Pallas kernels, per_device(): pl.pallas_call(kernel, out_shape=results, in_specs=[hbm] * 5, out_specs=(...  61.4 us
    unnamed x10, local copies, waits for them, and re-layouts  3.78 us

profile of v2, /device:TPU:1, one launch (start us, length us, event | category | flops | bytes accessed | tf_op | source)
XLA Modules:
  0.0 131.6 jit_solution(12852474192146437787)
XLA Ops:
  0.6 61.4 %shard_map.92 = (bf16[2,4,1024]{2,1,0:T(4,128)(2,1)S(1)}, bf16[2,4,1024]{2,1,0:T(4,128)(2,1)S(1)}, bf16[1024,512]{1,0:T(8,128)(2,1)S(1)}, bf16[512,1024]{1,0:T(8,128)(2,1)S(1)}, f32[1,1024]{1,0:T(1,128)S(1)}) custom-call(bf16[2,128,1024]{2,1,0:T(8,128)(2,1)} %x_hbm.1, f32[1,1024]{1,0:T(1,128)} %bitcast.2, bf16[1024,512]{1,0:T(8,128)(2,1)} %w1_hbm.1, ...), custom_call_target="tpu_custom_call" | custom-call | tf_op jit(solution)/shard_map/pallas_call | solution.py:503
  62.0 0.0 copy-start
  62.0 1.0 copy-done
  63.0 0.0 copy-start.1
  63.0 1.0 copy-done.1
  64.0 0.0 copy-start.2
  64.0 0.6 copy-done.2
  64.6 0.0 copy-start.3
  64.6 0.6 copy-done.3
  65.2 0.0 copy-start.4
  65.2 0.6 copy-done.4
  65.8 65.8 %shard_map.93 = (bf16[2,4,1024]{2,1,0:T(4,128)(2,1)}, bf16[2,4,1024]{2,1,0:T(4,128)(2,1)}, bf16[1024,512]{1,0:T(8,128)(2,1)}, bf16[512,1024]{1,0:T(8,128)(2,1)}, f32[1,1024]{1,0:T(1,128)}) custom-call(bf16[2,4,1024]{2,1,0:T(4,128)(2,1)} %copy-done.2, bf16[2,4,1024]{2,1,0:T(4,128)(2,1)} %copy-done.3, bf16[1024,512]{1,0:T(8,128)(2,1)} %copy-done, ...), custom_call_target="tpu_custom_call" | custom-call | tf_op jit(solution)/shard_map/pallas_call | solution.py:523
Async XLA Ops:
  62.0 1.0 copy-start
  63.0 1.0 copy-start.1
  64.0 0.6 copy-start.2
  64.6 0.6 copy-start.3
  65.2 0.6 copy-start.4

commit v3 on v2

--- a/solution.py
+++ b/solution.py
@@ -19,46 +19,53 @@
 
 
 class Phase:
-    def __init__(self, make, first, last, sems):
-        self.make, self.first, self.last, self.sems = make, first, last, sems
-        self.base = sems["used"]
-        sems["used"] += last - first
-
-    def copy(self, k):
-        src, dst, device = self.make(k)
-        place = self.base + k - self.first
+    def __init__(self, make, first, last, sems, whole=None):
+        self.make, self.first, self.last, self.sems, self.whole = make, first, last, sems, whole
+        self.place = sems["used"]
+        sems["used"] += 1
+
+    def describe(self, src, dst, device):
         return pltpu.make_async_remote_copy(
             src_ref=src,
             dst_ref=dst,
-            send_sem=self.sems["send"].at[place],
-            recv_sem=self.sems["recv"].at[place],
+            send_sem=self.sems["send"].at[self.send_place],
+            recv_sem=self.sems["recv"].at[self.place],
             device_id=device,
             device_id_type=MESH,
         )
 
-    def _each(self, what):
-        if self.last - self.first == 1:
-            what(self.copy(self.first))
+    def start(self):
+        order = self.sems["phases"]
+        self.send_place = len(order) % SENDS
+        if len(order) >= SENDS:
+            order[-SENDS].sent()
+        order.append(self)
+        if self.last - self.first <= 4:
+            for k in range(self.first, self.last):
+                self.describe(*self.make(k)).start()
             return
 
         def body(k, carry):
-            what(self.copy(k))
+            self.describe(*self.make(k)).start()
             return carry
 
         lax.fori_loop(self.first, self.last, body, 0)
 
-    def start(self):
-        self.sems["phases"].append(self)
-        self._each(lambda c: c.start())
+    def all(self):
+        src, dst, device = self.make(self.first)
+        if self.whole is not None:
+            src = dst = self.whole
+        return self.describe(src, dst, device)
 
     def arrived(self):
-        self._each(lambda c: c.wait_recv())
+        self.all().wait_recv()
 
     def sent(self):
-        self._each(lambda c: c.wait_send())
-
-
-COPIES = 160
+        self.all().wait_send()
+
+
+SENDS = 16
+PHASES = 40
 
 
 def kernel(
@@ -128,7 +135,7 @@
 
     to_xh = Phase(lambda k: (cg.at[mine], cg.at[other], xh_peer), 0, 1, sems)
     to_xh.start()
-    to_z = Phase(lambda k: (cg.at[mine], cg.at[mine], z_peer(k)), 1, N, sems)
+    to_z = Phase(lambda k: (cg.at[mine], cg.at[mine], z_peer(k)), 1, N, sems, cg.at[pl.ds(0, N - 1)])
     to_z.start()
 
     row = lax.broadcasted_iota(jnp.int32, (256, 256), 0)
@@ -150,7 +157,7 @@
         .astype(BF16)
         .reshape(2, 128, HID)
     )
-    a_y = Phase(lambda k: (s_a.at[:, y_rows(k)], r_a.at[k], y_peer(k)), 1, N, sems)
+    a_y = Phase(lambda k: (s_a.at[:, y_rows(k)], r_a.at[k], y_peer(k)), 1, N, sems, r_a.at[pl.ds(1, N - 1)])
     a_y.start()
 
     ones = jnp.ones((8, FEAT), BF16)
@@ -166,11 +173,11 @@
         )
     place = lax.broadcasted_iota(jnp.int32, (8, 128), 0)
     s_sq[...] = jnp.where(place == 0, squares[0], squares[1])
-    sq_y = Phase(lambda k: (s_sq, r_sq.at[k], y_peer(k)), 1, N, sems)
+    sq_y = Phase(lambda k: (s_sq, r_sq.at[k], y_peer(k)), 1, N, sems, r_sq.at[pl.ds(1, N - 1)])
     sq_y.start()
 
     to_xh.arrived()
-    to_z2 = Phase(lambda k: (cg.at[other], cg.at[other], z_peer(k)), 1, N, sems)
+    to_z2 = Phase(lambda k: (cg.at[other], cg.at[other], z_peer(k)), 1, N, sems, cg.at[pl.ds(0, N - 1)])
     to_z2.start()
     core_rows = pl.ds(pl.multiple_of(64 * c, 64), 64)
     u_lo = Phase(lambda k: (u.at[:, core_rows], u_o.at[:, core_rows], lo_peer), 0, 1, sems)
@@ -189,7 +196,13 @@
         return pieces_ref[h * 16 : (h + 1) * 16].astype(F32).reshape(128, FEAT).astype(BF16)
 
     c_y = [
-        Phase(lambda k, h=h: (s_c.at[h, y_rows(k)], r_c.at[k, h], y_peer(k)), 1, N, sems)
+        Phase(
+            lambda k, h=h: (s_c.at[h, y_rows(k)], r_c.at[h, k], y_peer(k)),
+            1,
+            N,
+            sems,
+            r_c.at[h, pl.ds(1, N - 1)],
+        )
         for h in range(2)
     ]
 
@@ -229,7 +242,11 @@
         scl[h] = jnp.broadcast_to(scale, (16, 128))
 
     b_near = Phase(
-        lambda k: (hid.at[:, my_rows], hid.at[:, my_rows], y_peer(1 + 6 * k)), 0, 2, sems
+        lambda k: (hid.at[:, my_rows], hid.at[:, my_rows], y_peer(1 + 6 * k)),
+        0,
+        2,
+        sems,
+        hid.at[:, pl.ds(0, 32)],
     )
     b_near.start()
 
@@ -242,32 +259,38 @@
     cot_lo0.start()
 
     b_near.arrived()
-    left_rows, right_rows = y_rows(N - 1), y_rows(1)
-    b_right = Phase(
-        lambda k: (hid.at[:, left_rows], hid.at[:, left_rows], y_peer(k)), 1, 3, sems
-    )
-    b_left = Phase(
-        lambda k: (hid.at[:, right_rows], hid.at[:, right_rows], y_peer(N - k)), 1, 3, sems
-    )
-    b_right3 = Phase(
-        lambda k: (hid.at[0, left_rows], hid.at[0, left_rows], y_peer(3)), 0, 1, sems
-    )
-    b_left3 = Phase(
-        lambda k: (hid.at[1, right_rows], hid.at[1, right_rows], y_peer(N - 3)), 0, 1, sems
-    )
-    b_rest = (b_right3, b_left3, b_right, b_left)
+
+    def pass_on(k):
+        side, step = k // 2, k % 2 + 1
+        rows = y_rows(1 if side else N - 1)
+        return hid.at[:, rows], hid.at[:, rows], y_peer(N - step if side else step)
+
+    def pass_far(k):
+        rows = y_rows(1 if k else N - 1)
+        return hid.at[k, rows], hid.at[k, rows], y_peer(N - 3 if k else 3)
+
+    b_rest = (
+        Phase(pass_far, 0, 2, sems, hid.at[0, pl.ds(0, 32)]),
+        Phase(pass_on, 0, 4, sems, hid.at[:, pl.ds(0, 64)]),
+    )
     for phase in b_rest:
         phase.start()
 
     d_y = [
-        Phase(lambda k, h=h: (q.at[h, my_rows], q.at[h, my_rows], y_peer(k)), 1, N, sems)
+        Phase(
+            lambda k, h=h: (q.at[h, my_rows], q.at[h, my_rows], y_peer(k)),
+            1,
+            N,
+            sems,
+            q.at[h, pl.ds(0, 16 * (N - 1))],
+        )
         for h in range(2)
     ]
     for h in (1, 0):
         c_y[h].arrived()
         sums = s_c[h, my_rows].astype(F32)
         for k in range(1, N):
-            sums = sums + r_c[k, h].astype(F32)
+            sums = sums + r_c[h, k].astype(F32)
         scale = scl[h][:, :1]
         own = sums * slope[h] * scale
         q[h, my_rows] = own.astype(BF16)
@@ -278,7 +301,7 @@
         e_s[:, h * 128 : (h + 1) * 128] = jnp.sum(
             jnp.where(lane == spot, inner, 0.0), axis=0, keepdims=True
         )
-    e_y = Phase(lambda k: (e_s, e_r.at[k], y_peer(k)), 1, N, sems)
+    e_y = Phase(lambda k: (e_s, e_r.at[k], y_peer(k)), 1, N, sems, e_r.at[pl.ds(1, N - 1)])
     e_y.start()
 
     for phase in b_rest:
@@ -301,7 +324,11 @@
         both = branch[h, core_rows] + r_fs[h]
         s_fz[h] = both.reshape(N, 8, FEAT).astype(BF16)
     f_z = Phase(
-        lambda k: (s_fz.at[:, z_place(k)], r_fz.at[k], z_peer(k)), 1, N, sems
+        lambda k: (s_fz.at[:, z_place(k)], r_fz.at[k], z_peer(k)),
+        1,
+        N,
+        sems,
+        r_fz.at[pl.ds(1, N - 1)],
     )
     f_z.start()
 
@@ -310,7 +337,13 @@
         for h in range(2)
     ]
     g_zs = [
-        Phase(lambda k, h=h: (s_gz.at[h, z_place(k)], r_gz.at[h, k], z_peer(k)), 1, N, sems)
+        Phase(
+            lambda k, h=h: (s_gz.at[h, z_place(k)], r_gz.at[h, k], z_peer(k)),
+            1,
+            N,
+            sems,
+            r_gz.at[h, pl.ds(1, N - 1)],
+        )
         for h in range(2)
     ]
     q_lo = [
@@ -342,7 +375,7 @@
         g_zs[h].start()
     gg_sib.arrived()
     gg_chip[...] = gg_own[...] + gg_r1[...]
-    gg_z = Phase(lambda k: (gg_chip, gg_rz.at[k], z_peer(k)), 1, N, sems)
+    gg_z = Phase(lambda k: (gg_chip, gg_rz.at[k], z_peer(k)), 1, N, sems, gg_rz.at[pl.ds(1, N - 1)])
     gg_z.start()
 
     cot_sibo = [
@@ -388,12 +421,9 @@
     for k in range(1, N):
         gg_total = gg_total + gg_rz[k]
     gg_line[...] = gg_total
-    gg_x = [
-        Phase(lambda k, i=i, peer=peer: (gg_line, gg_rx.at[i], peer), 0, 1, sems)
-        for i, peer in enumerate((xh_peer, lo_peer, far_peer))
-    ]
-    for phase in gg_x:
-        phase.start()
+    x_peers = (xh_peer, lo_peer, far_peer)
+    gg_x = Phase(lambda k: (gg_line, gg_rx.at[k], x_peers[k]), 0, 3, sems, gg_rx)
+    gg_x.start()
 
     u_sib.arrived()
     for h in range(2):
@@ -414,8 +444,7 @@
     normed_grad = z_total(s_gz, lambda k: r_gz[1, k].astype(F32), 1)
     g_xh.arrived()
     normed_grad = normed_grad + r_gx[...]
-    for phase in gg_x:
-        phase.arrived()
+    gg_x.arrived()
     inner_row = gg_line[:, FEAT + 128 : ROW] + gg_rx[0][:, FEAT : FEAT + 128]
     own_lane = lax.broadcasted_iota(jnp.int32, (8, 128), 1)
     own_spot = lax.broadcasted_iota(jnp.int32, (8, 128), 0) + c * 64 + z * 8
@@ -431,7 +460,7 @@
         gg_rx[1][:, 0:FEAT] + gg_rx[2][:, 0:FEAT]
     )
 
-    for phase in sems["phases"]:
+    for phase in sems["phases"][-SENDS:]:
         phase.sent()
 
 
@@ -464,7 +493,7 @@
         ((8, 128), F32),
         ((N, 8, 128), F32),
         ((2, 128, HID), BF16),
-        ((N, 2, 16, HID), BF16),
+        ((2, N, 16, HID), BF16),
         ((2, 128, HID), BF16),
         ((2, 128, HID), BF16),
         ((2, 128, HID), BF16),
@@ -507,8 +536,8 @@
         out_specs=(vmem,) * 5,
         scratch_shapes=[pltpu.VMEM(shape, dtype) for shape, dtype in shapes]
         + [
-            pltpu.SemaphoreType.DMA((COPIES,)),
-            pltpu.SemaphoreType.DMA((COPIES,)),
+            pltpu.SemaphoreType.DMA((SENDS,)),
+            pltpu.SemaphoreType.DMA((PHASES,)),
             pltpu.SemaphoreType.DMA((5,)),
         ],
         compiler_params=pltpu.CompilerParams(
@@ -523,8 +552,8 @@
     outputs, input_grad, first_grad, second_grad, gain_grad = pl.pallas_call(
         save,
         out_shape=results,
-        in_specs=[anywhere] * 5,
-        out_specs=(hbm,) * 5,
+        in_specs=[vmem] * 5,
+        out_specs=(anywhere,) * 5,
         scratch_shapes=[pltpu.SemaphoreType.DMA((5,))],
     )(*made)
     return outputs, input_grad, first_grad, second_grad, gain_grad.reshape(FEAT)

time: 132 us -> 65.5 us (0.50)
  Pallas kernels: 127 us -> 60.9 us
    pallas_call x1, Pallas kernels: 65.8 us -> 2.94 us  [per_device(): pl.pallas_call(save, out_shape=results, in_specs=[vmem] * 5, out_specs=(a...]
    pallas_call x1, Pallas kernels: 61.4 us -> 57.9 us  [per_device(): pl.pallas_call(kernel, out_shape=results, in_specs=[hbm] * 5, out_specs=(...]
where the time goes in v3:
time: 65.5 us; the launch traced here: 65.3 us
  Pallas kernels  60.9 us (93%)
  local copies, waits for them, and re-layouts  3.78 us (6%)
    pallas_call x1, Pallas kernels, per_device(): pl.pallas_call(kernel, out_shape=results, in_specs=[hbm] * 5, out_specs=(...  57.9 us
    unnamed x10, local copies, waits for them, and re-layouts  3.78 us
    pallas_call x1, Pallas kernels, per_device(): pl.pallas_call(save, out_shape=results, in_specs=[vmem] * 5, out_specs=(a...  2.94 us

profile of v3, /device:TPU:1, one launch (start us, length us, event | category | flops | bytes accessed | tf_op | source)
XLA Modules:
  0.0 65.3 jit_solution(15676480905819894912)
XLA Ops:
  0.6 57.9 %shard_map.92 = (bf16[2,4,1024]{2,1,0:T(4,128)(2,1)S(1)}, bf16[2,4,1024]{2,1,0:T(4,128)(2,1)S(1)}, bf16[1024,512]{1,0:T(8,128)(2,1)S(1)}, bf16[512,1024]{1,0:T(8,128)(2,1)S(1)}, f32[1,1024]{1,0:T(1,128)S(1)}) custom-call(bf16[2,128,1024]{2,1,0:T(8,128)(2,1)} %x_hbm.1, f32[1,1024]{1,0:T(1,128)} %bitcast.2, bf16[1024,512]{1,0:T(8,128)(2,1)} %w1_hbm.1, ...), custom_call_target="tpu_custom_call" | custom-call | tf_op jit(solution)/shard_map/pallas_call | solution.py:532
  58.6 0.0 copy-start
  58.6 1.0 %copy-done = bf16[1024,512]{1,0:T(8,128)(2,1)} copy-done((bf16[1024,512]{1,0:T(8,128)(2,1)}, bf16[1024,512]{1,0:T(8,128)(2,1)S(1)}, u32[]{:S(2)}) %copy-start) | copy-done | bytes 1048600
  59.5 0.0 copy-start.1
  59.5 1.0 %copy-done.1 = bf16[512,1024]{1,0:T(8,128)(2,1)} copy-done((bf16[512,1024]{1,0:T(8,128)(2,1)}, bf16[512,1024]{1,0:T(8,128)(2,1)S(1)}, u32[]{:S(2)}) %copy-start.1) | copy-done | bytes 1048600
  60.6 0.0 copy-start.2
  60.6 0.6 copy-done.2
  61.2 0.0 copy-start.3
  61.2 0.6 copy-done.3
  61.8 0.0 copy-start.4
  61.8 0.6 copy-done.4
  62.4 2.9 %shard_map.93 = (bf16[2,4,1024]{2,1,0:T(4,128)(2,1)}, bf16[2,4,1024]{2,1,0:T(4,128)(2,1)}, bf16[1024,512]{1,0:T(8,128)(2,1)}, bf16[512,1024]{1,0:T(8,128)(2,1)}, f32[1,1024]{1,0:T(1,128)}) custom-call(bf16[2,4,1024]{2,1,0:T(4,128)(2,1)} %copy-done.2, bf16[2,4,1024]{2,1,0:T(4,128)(2,1)} %copy-done.3, bf16[1024,512]{1,0:T(8,128)(2,1)} %copy-done, ...), custom_call_target="tpu_custom_call" | custom-call | tf_op jit(solution)/shard_map/pallas_call | solution.py:552
Async XLA Ops:
  58.6 1.0 %copy-start = (bf16[1024,512]{1,0:T(8,128)(2,1)}, bf16[1024,512]{1,0:T(8,128)(2,1)S(1)}, u32[]{:S(2)}) copy-start(bf16[1024,512]{1,0:T(8,128)(2,1)S(1)} %get-tuple-element.17.refs_2_) | copy-start | bytes 3145732
  59.5 1.0 %copy-start.1 = (bf16[512,1024]{1,0:T(8,128)(2,1)}, bf16[512,1024]{1,0:T(8,128)(2,1)S(1)}, u32[]{:S(2)}) copy-start(bf16[512,1024]{1,0:T(8,128)(2,1)S(1)} %get-tuple-element.18.refs_3_) | copy-start | bytes 3145732
  60.6 0.6 copy-start.2
  61.2 0.6 copy-start.3
  61.8 0.6 copy-start.4

commit v4 on v3

--- a/solution.py
+++ b/solution.py
@@ -65,7 +65,8 @@
 
 
 SENDS = 16
-PHASES = 40
+FAR = (1, N - 1, 3, N - 3)
+PHASES = 37
 
 
 def kernel(
@@ -73,7 +74,7 @@
     out_ref, ing_ref, first_out, second_out, gg_ref,
     x_in, gain_ref, w1, w2, cot_ref, xp, u, u_o, cg, cg_o,
     s_a, r_a, s_sq, r_sq, s_c, r_c, hid, hid_o, q, q_o, p_own, slope, scl,
-    branch, r_fs, s_fz, r_fz, s_fx, r_fx,
+    branch, r_fs, s_fz, r_fz, r_ff, r_f2, s_fx, r_fx,
     big, r_gs, s_gz, r_gz, s_gx, r_gx,
     e_s, e_r, gg_own, gg_r1, gg_chip, gg_rz, gg_line, gg_rx,
     send_sems, recv_sems, local_sems,
@@ -130,13 +131,6 @@
     load_cot.wait()
     cot_own = jnp.concatenate([cot_ref[0].astype(F32), cot_ref[1].astype(F32)], axis=0)
     cg[mine] = cot_own.astype(BF16)
-
-    pl.semaphore_wait(barrier, 2 * (N - 1) + 4)
-
-    to_xh = Phase(lambda k: (cg.at[mine], cg.at[other], xh_peer), 0, 1, sems)
-    to_xh.start()
-    to_z = Phase(lambda k: (cg.at[mine], cg.at[mine], z_peer(k)), 1, N, sems, cg.at[pl.ds(0, N - 1)])
-    to_z.start()
 
     row = lax.broadcasted_iota(jnp.int32, (256, 256), 0)
     col = lax.broadcasted_iota(jnp.int32, (256, 256), 1)
@@ -157,8 +151,13 @@
         .astype(BF16)
         .reshape(2, 128, HID)
     )
+    pl.semaphore_wait(barrier, 2 * (N - 1) + 4)
     a_y = Phase(lambda k: (s_a.at[:, y_rows(k)], r_a.at[k], y_peer(k)), 1, N, sems, r_a.at[pl.ds(1, N - 1)])
     a_y.start()
+    to_xh = Phase(lambda k: (cg.at[mine], cg.at[other], xh_peer), 0, 1, sems)
+    to_xh.start()
+    to_z = Phase(lambda k: (cg.at[mine], cg.at[mine], z_peer(k)), 1, N, sems, cg.at[pl.ds(0, N - 1)])
+    to_z.start()
 
     ones = jnp.ones((8, FEAT), BF16)
     squares = []
@@ -323,14 +322,17 @@
     for h in range(2):
         both = branch[h, core_rows] + r_fs[h]
         s_fz[h] = both.reshape(N, 8, FEAT).astype(BF16)
-    f_z = Phase(
-        lambda k: (s_fz.at[:, z_place(k)], r_fz.at[k], z_peer(k)),
-        1,
-        N,
-        sems,
-        r_fz.at[pl.ds(1, N - 1)],
-    )
-    f_z.start()
+
+    def f_near(k):
+        step = N - 1 if k % 2 else 1
+        if k < 2:
+            return s_fz.at[:, z_place(2 * step)], r_fz.at[k], z_peer(step)
+        return s_fz.at[k - 2, z_place(4)], r_ff.at[k - 2], z_peer(step)
+
+    f_one = Phase(f_near, 0, 2, sems, r_fz)
+    f_one.start()
+    f_four = Phase(lambda k: f_near(k + 2), 0, 2, sems, r_ff)
+    f_four.start()
 
     g_sibs = [
         Phase(lambda k, h=h: (big.at[h, sib_rows], r_gs.at[h], sib_peer), 0, 1, sems)
@@ -350,15 +352,32 @@
         Phase(lambda k, h=h: (q.at[h], q_o.at[h], lo_peer), 0, 1, sems)
         for h in range(2)
     ]
+    f_far = Phase(
+        lambda k: (s_fz.at[:, z_place(FAR[k])], r_f2.at[k], z_peer(FAR[k])), 0, 4, sems, r_f2
+    )
+
+    def pass_f():
+        f_one.arrived()
+        f_four.arrived()
+        for k, step in ((0, 1), (1, N - 1)):
+            to = z_place(step)
+            for h in range(2):
+                s_fz[h, to] = (s_fz[h, to].astype(F32) + r_fz[k, h].astype(F32)).astype(BF16)
+            to = z_place(3 * step)
+            s_fz[k, to] = (s_fz[k, to].astype(F32) + r_ff[k].astype(F32)).astype(BF16)
+        f_far.start()
+
     gain_part = jnp.zeros((1, FEAT), F32)
     for h in range(2):
         d_y[h].arrived()
-        part = lax.dot_general(q[h], w1[...], NT, preferred_element_type=F32)
-        big[h] = part
-        g_sibs[h].start()
+        for rows in (sib_rows, core_rows):
+            part = lax.dot_general(q[h, rows], w1[...], NT, preferred_element_type=F32)
+            big[h, rows] = part
+            if rows is sib_rows:
+                g_sibs[h].start()
         q_lo[h].start()
         gain_part = gain_part + jnp.sum(
-            part * xp[h * 128 : (h + 1) * 128, :], axis=0, keepdims=True
+            big[h] * xp[h * 128 : (h + 1) * 128, :], axis=0, keepdims=True
         )
         if h == 1:
             e_y.arrived()
@@ -372,11 +391,16 @@
         g_sibs[h].arrived()
         both = big[h, core_rows] + r_gs[h]
         s_gz[h] = both.reshape(N, 8, FEAT).astype(BF16)
+        if h == 1:
+            gg_sib.arrived()
+            gg_chip[...] = gg_own[...] + gg_r1[...]
+            gg_z = Phase(
+                lambda k: (gg_chip, gg_rz.at[k], z_peer(k)), 1, N, sems, gg_rz.at[pl.ds(1, N - 1)]
+            )
+            gg_z.start()
         g_zs[h].start()
-    gg_sib.arrived()
-    gg_chip[...] = gg_own[...] + gg_r1[...]
-    gg_z = Phase(lambda k: (gg_chip, gg_rz.at[k], z_peer(k)), 1, N, sems, gg_rz.at[pl.ds(1, N - 1)])
-    gg_z.start()
+        if h == 0:
+            pass_f()
 
     cot_sibo = [
         Phase(lambda k, h=h: (cg_o.at[pieces(h)], cg_o.at[pieces(h)], sib_peer), 0, 1, sems)
@@ -405,11 +429,17 @@
             total = total + received(k)
         return total
 
-    f_z.arrived()
-    s_fx[...] = z_total(s_fz, lambda k: r_fz[k, 0].astype(F32), 0)
+    def f_total(h):
+        total = s_fz[h, z].astype(F32)
+        for k in range(4):
+            total = total + r_f2[k, h].astype(F32)
+        return total
+
+    f_far.arrived()
+    s_fx[...] = f_total(0)
     f_xh = Phase(lambda k: (s_fx, r_fx, xh_peer), 0, 1, sems)
     f_xh.start()
-    own_branch = z_total(s_fz, lambda k: r_fz[k, 1].astype(F32), 1)
+    own_branch = f_total(1)
 
     g_zs[0].arrived()
     s_gx[...] = z_total(s_gz, lambda k: r_gz[0, k].astype(F32), 0)
@@ -504,7 +534,9 @@
         ((2, 128, FEAT), F32),
         ((2, 64, FEAT), F32),
         ((2, N, 8, FEAT), BF16),
-        ((N, 2, 8, FEAT), BF16),
+        ((2, 2, 8, FEAT), BF16),
+        ((2, 8, FEAT), BF16),
+        ((4, 2, 8, FEAT), BF16),
         ((8, FEAT), F32),
         ((8, FEAT), F32),
         ((2, 128, FEAT), F32),

time: 65.5 us -> 62.7 us (0.957)
  Pallas kernels: 60.9 us -> 58.1 us
    pallas_call x1, Pallas kernels: 57.9 us -> 55.1 us  [per_device(): pl.pallas_call(kernel, out_shape=results, in_specs=[hbm] * 5, out_specs=(...]
where the time goes in v4:
time: 62.7 us; the launch traced here: 62.5 us
  Pallas kernels  58.1 us (93%)
  local copies, waits for them, and re-layouts  3.78 us (6%)
  between operations  0.65 us (1%)
    pallas_call x1, Pallas kernels, per_device(): pl.pallas_call(kernel, out_shape=results, in_specs=[hbm] * 5, out_specs=(...  55.1 us
    unnamed x10, local copies, waits for them, and re-layouts  3.78 us
    pallas_call x1, Pallas kernels, per_device(): pl.pallas_call(save, out_shape=results, in_specs=[vmem] * 5, out_specs=(a...  2.94 us

profile of v4, /device:TPU:1, one launch (start us, length us, event | category | flops | bytes accessed | tf_op | source)
XLA Modules:
  0.0 62.5 jit_solution(3986789250533142231)
XLA Ops:
  0.6 55.1 %shard_map.92 = (bf16[2,4,1024]{2,1,0:T(4,128)(2,1)S(1)}, bf16[2,4,1024]{2,1,0:T(4,128)(2,1)S(1)}, bf16[1024,512]{1,0:T(8,128)(2,1)S(1)}, bf16[512,1024]{1,0:T(8,128)(2,1)S(1)}, f32[1,1024]{1,0:T(1,128)S(1)}) custom-call(bf16[2,128,1024]{2,1,0:T(8,128)(2,1)} %x_hbm.1, f32[1,1024]{1,0:T(1,128)} %bitcast.2, bf16[1024,512]{1,0:T(8,128)(2,1)} %w1_hbm.1, ...), custom_call_target="tpu_custom_call" | custom-call | tf_op jit(solution)/shard_map/pallas_call | solution.py:564
  55.8 0.0 copy-start
  55.8 1.0 %copy-done = bf16[1024,512]{1,0:T(8,128)(2,1)} copy-done((bf16[1024,512]{1,0:T(8,128)(2,1)}, bf16[1024,512]{1,0:T(8,128)(2,1)S(1)}, u32[]{:S(2)}) %copy-start) | copy-done | bytes 1048600
  56.8 0.0 copy-start.1
  56.8 1.0 %copy-done.1 = bf16[512,1024]{1,0:T(8,128)(2,1)} copy-done((bf16[512,1024]{1,0:T(8,128)(2,1)}, bf16[512,1024]{1,0:T(8,128)(2,1)S(1)}, u32[]{:S(2)}) %copy-start.1) | copy-done | bytes 1048600
  57.8 0.0 copy-start.2
  57.8 0.6 copy-done.2
  58.4 0.0 copy-start.3
  58.4 0.6 copy-done.3
  59.0 0.0 copy-start.4
  59.0 0.6 copy-done.4
  59.6 2.9 %shard_map.93 = (bf16[2,4,1024]{2,1,0:T(4,128)(2,1)}, bf16[2,4,1024]{2,1,0:T(4,128)(2,1)}, bf16[1024,512]{1,0:T(8,128)(2,1)}, bf16[512,1024]{1,0:T(8,128)(2,1)}, f32[1,1024]{1,0:T(1,128)}) custom-call(bf16[2,4,1024]{2,1,0:T(4,128)(2,1)} %copy-done.2, bf16[2,4,1024]{2,1,0:T(4,128)(2,1)} %copy-done.3, bf16[1024,512]{1,0:T(8,128)(2,1)} %copy-done, ...), custom_call_target="tpu_custom_call" | custom-call | tf_op jit(solution)/shard_map/pallas_call | solution.py:584
Async XLA Ops:
  55.8 1.0 %copy-start = (bf16[1024,512]{1,0:T(8,128)(2,1)}, bf16[1024,512]{1,0:T(8,128)(2,1)S(1)}, u32[]{:S(2)}) copy-start(bf16[1024,512]{1,0:T(8,128)(2,1)S(1)} %get-tuple-element.17.refs_2_) | copy-start | bytes 3145732
  56.8 1.0 %copy-start.1 = (bf16[512,1024]{1,0:T(8,128)(2,1)}, bf16[512,1024]{1,0:T(8,128)(2,1)S(1)}, u32[]{:S(2)}) copy-start(bf16[512,1024]{1,0:T(8,128)(2,1)S(1)} %get-tuple-element.18.refs_3_) | copy-start | bytes 3145732
  57.8 0.6 copy-start.2
  58.4 0.6 copy-start.3
  59.0 0.6 copy-start.4

commit v5 on v4

--- a/solution.py
+++ b/solution.py
@@ -13,7 +13,6 @@
 N = 8
 HID = 512
 FEAT = 1024
-ROW = FEAT + 256
 NT = (((1,), (1,)), ((), ()))
 TN = (((0,), (0,)), ((), ()))
 
@@ -35,21 +34,14 @@
         )
 
     def start(self):
-        order = self.sems["phases"]
-        self.send_place = len(order) % SENDS
-        if len(order) >= SENDS:
-            order[-SENDS].sent()
-        order.append(self)
-        if self.last - self.first <= 4:
-            for k in range(self.first, self.last):
-                self.describe(*self.make(k)).start()
-            return
-
-        def body(k, carry):
+        phases = self.sems["phases"]
+        self.send_place = len(phases) % SENDS
+        if len(phases) >= SENDS:
+            phases[-SENDS].sent()
+        phases.append(self)
+        order = FARTHEST_FIRST if self.last == N else range(self.first, self.last)
+        for k in order:
             self.describe(*self.make(k)).start()
-            return carry
-
-        lax.fori_loop(self.first, self.last, body, 0)
 
     def all(self):
         src, dst, device = self.make(self.first)
@@ -65,8 +57,9 @@
 
 
 SENDS = 16
-FAR = (1, N - 1, 3, N - 3)
-PHASES = 37
+FAR = (3, N - 3, 1, N - 1)
+FARTHEST_FIRST = (3, 5, 4, 2, 6, 1, 7)
+PHASES = 40
 
 
 def kernel(
@@ -76,7 +69,7 @@
     s_a, r_a, s_sq, r_sq, s_c, r_c, hid, hid_o, q, q_o, p_own, slope, scl,
     branch, r_fs, s_fz, r_fz, r_ff, r_f2, s_fx, r_fx,
     big, r_gs, s_gz, r_gz, s_gx, r_gx,
-    e_s, e_r, gg_own, gg_r1, gg_chip, gg_rz, gg_line, gg_rx,
+    e_s, e_r, ee_own, ee_r1, ee_chip, ee_rz, ee_line, ee_rx, gg_own, gg_r1, gg_chip, gg_rz, gg_line, gg_rx,
     send_sems, recv_sems, local_sems,
 ):
     s = lax.axis_index("section")
@@ -295,13 +288,13 @@
         q[h, my_rows] = own.astype(BF16)
         if h == 0:
             d_y[0].start()
-            d_y[1].start()
         inner = jnp.sum(own * p_own[h], axis=1, keepdims=True) * (scale * scale / D)
         e_s[:, h * 128 : (h + 1) * 128] = jnp.sum(
             jnp.where(lane == spot, inner, 0.0), axis=0, keepdims=True
         )
     e_y = Phase(lambda k: (e_s, e_r.at[k], y_peer(k)), 1, N, sems, e_r.at[pl.ds(1, N - 1)])
     e_y.start()
+    d_y[1].start()
 
     for phase in b_rest:
         phase.arrived()
@@ -367,6 +360,8 @@
             s_fz[k, to] = (s_fz[k, to].astype(F32) + r_ff[k].astype(F32)).astype(BF16)
         f_far.start()
 
+    ee_sib = Phase(lambda k: (ee_own, ee_r1, sib_peer), 0, 1, sems)
+    ee_z = Phase(lambda k: (ee_chip, ee_rz.at[k], z_peer(k)), 1, N, sems, ee_rz.at[pl.ds(1, N - 1)])
     gain_part = jnp.zeros((1, FEAT), F32)
     for h in range(2):
         d_y[h].arrived()
@@ -375,17 +370,21 @@
             big[h, rows] = part
             if rows is sib_rows:
                 g_sibs[h].start()
-        q_lo[h].start()
-        gain_part = gain_part + jnp.sum(
-            big[h] * xp[h * 128 : (h + 1) * 128, :], axis=0, keepdims=True
-        )
-        if h == 1:
+        if h == 0:
             e_y.arrived()
             e_sum = e_s[...]
             for k in range(1, N):
                 e_sum = e_sum + e_r[k]
-            gg_own[:, 0:FEAT] = gain_part
-            gg_own[:, FEAT:ROW] = e_sum
+            ee_own[...] = e_sum
+            ee_sib.start()
+        q_lo[h].start()
+        gain_part = gain_part + jnp.sum(
+            big[h] * xp[h * 128 : (h + 1) * 128, :], axis=0, keepdims=True
+        )
+        if h == 0:
+            pass_f()
+        else:
+            gg_own[...] = gain_part
             gg_sib = Phase(lambda k: (gg_own, gg_r1, sib_peer), 0, 1, sems)
             gg_sib.start()
         g_sibs[h].arrived()
@@ -400,7 +399,9 @@
             gg_z.start()
         g_zs[h].start()
         if h == 0:
-            pass_f()
+            ee_sib.arrived()
+            ee_chip[...] = ee_own[...] + ee_r1[...]
+            ee_z.start()
 
     cot_sibo = [
         Phase(lambda k, h=h: (cg_o.at[pieces(h)], cg_o.at[pieces(h)], sib_peer), 0, 1, sems)
@@ -435,6 +436,14 @@
             total = total + r_f2[k, h].astype(F32)
         return total
 
+    ee_z.arrived()
+    ee_total = ee_chip[...]
+    for k in range(1, N):
+        ee_total = ee_total + ee_rz[k]
+    ee_line[...] = ee_total
+    ee_xh = Phase(lambda k: (ee_line, ee_rx, xh_peer), 0, 1, sems)
+    ee_xh.start()
+
     f_far.arrived()
     s_fx[...] = f_total(0)
     f_xh = Phase(lambda k: (s_fx, r_fx, xh_peer), 0, 1, sems)
@@ -474,8 +483,8 @@
     normed_grad = z_total(s_gz, lambda k: r_gz[1, k].astype(F32), 1)
     g_xh.arrived()
     normed_grad = normed_grad + r_gx[...]
-    gg_x.arrived()
-    inner_row = gg_line[:, FEAT + 128 : ROW] + gg_rx[0][:, FEAT : FEAT + 128]
+    ee_xh.arrived()
+    inner_row = ee_line[:, 128:256] + ee_rx[:, 0:128]
     own_lane = lax.broadcasted_iota(jnp.int32, (8, 128), 1)
     own_spot = lax.broadcasted_iota(jnp.int32, (8, 128), 0) + c * 64 + z * 8
     inner = jnp.sum(
@@ -486,9 +495,8 @@
     grads = cg[mine].astype(F32) + gain * normed_grad - x_own * inner
     ing_ref[0] = grads[0:4].astype(BF16)
     ing_ref[1] = grads[4:8].astype(BF16)
-    gg_ref[...] = (gg_line[:, 0:FEAT] + gg_rx[0][:, 0:FEAT]) + (
-        gg_rx[1][:, 0:FEAT] + gg_rx[2][:, 0:FEAT]
-    )
+    gg_x.arrived()
+    gg_ref[...] = (gg_line[...] + gg_rx[0]) + (gg_rx[1] + gg_rx[2])
 
     for phase in sems["phases"][-SENDS:]:
         phase.sent()
@@ -547,12 +555,18 @@
         ((8, FEAT), F32),
         ((1, 256), F32),
         ((N, 1, 256), F32),
-        ((1, ROW), F32),
-        ((1, ROW), F32),
-        ((1, ROW), F32),
-        ((N, 1, ROW), F32),
-        ((1, ROW), F32),
-        ((3, 1, ROW), F32),
+        ((1, 256), F32),
+        ((1, 256), F32),
+        ((1, 256), F32),
+        ((N, 1, 256), F32),
+        ((1, 256), F32),
+        ((1, 256), F32),
+        ((1, FEAT), F32),
+        ((1, FEAT), F32),
+        ((1, FEAT), F32),
+        ((N, 1, FEAT), F32),
+        ((1, FEAT), F32),
+        ((3, 1, FEAT), F32),
     ]
     results = (
         jax.ShapeDtypeStruct(cotangent.shape, BF16),
@@ -587,7 +601,8 @@
         in_specs=[vmem] * 5,
         out_specs=(anywhere,) * 5,
         scratch_shapes=[pltpu.SemaphoreType.DMA((5,))],
-    )(*made)
+        compiler_params=pltpu.CompilerParams(vmem_limit_bytes=4 * 1024 * 1024),
+    )(*(pltpu.with_memory_space_constraint(array, pltpu.VMEM) for array in made))
     return outputs, input_grad, first_grad, second_grad, gain_grad.reshape(FEAT)
 
 

time: 62.7 us -> 56.8 us (0.906); the launches traced: 62.5 us -> 55.9 us
  local copies, waits for them, and re-layouts: 3.78 us -> 0 us
  Pallas kernels: 58.1 us -> 55.2 us
    unnamed x10 -> x0, local copies, waits for them, and re-layouts: 3.78 us -> none
    pallas_call x1, Pallas kernels: 2.94 us -> 1.38 us  [per_device(): pl.pallas_call(save, out_shape=results, in_specs=[vmem] * 5, out_specs=(a...]
    pallas_call x1, Pallas kernels: 55.1 us -> 53.9 us  [per_device(): pl.pallas_call(kernel, out_shape=results, in_specs=[hbm] * 5, out_specs=(...]
where the time goes in v5:
time: 56.8 us; the launch traced here: 55.9 us
  Pallas kernels  55.2 us (97%)
  between operations  0.64 us (1%)
    pallas_call x1, Pallas kernels, per_device(): pl.pallas_call(kernel, out_shape=results, in_specs=[hbm] * 5, out_specs=(...  53.9 us
    pallas_call x1, Pallas kernels, per_device(): pl.pallas_call(save, out_shape=results, in_specs=[vmem] * 5, out_specs=(a...  1.38 us

profile of v5, /device:TPU:1, one launch (start us, length us, event | category | flops | bytes accessed | tf_op | source)
XLA Modules:
  0.0 55.9 jit_solution(6429735299306834288)
XLA Ops:
  0.6 53.9 %shard_map.92 = (bf16[2,4,1024]{2,1,0:T(4,128)(2,1)S(1)}, bf16[2,4,1024]{2,1,0:T(4,128)(2,1)S(1)}, bf16[1024,512]{1,0:T(8,128)(2,1)S(1)}, bf16[512,1024]{1,0:T(8,128)(2,1)S(1)}, f32[1,1024]{1,0:T(1,128)S(1)}) custom-call(bf16[2,128,1024]{2,1,0:T(8,128)(2,1)} %x_hbm.1, f32[1,1024]{1,0:T(1,128)} %bitcast.2, bf16[1024,512]{1,0:T(8,128)(2,1)} %w1_hbm.1, ...), custom_call_target="tpu_custom_call" | custom-call | tf_op jit(solution)/shard_map/pallas_call | solution.py:578
  54.5 1.4 %shard_map.93 = (bf16[2,4,1024]{2,1,0:T(4,128)(2,1)}, bf16[2,4,1024]{2,1,0:T(4,128)(2,1)}, bf16[1024,512]{1,0:T(8,128)(2,1)}, bf16[512,1024]{1,0:T(8,128)(2,1)}, f32[1,1024]{1,0:T(1,128)}) custom-call(bf16[2,4,1024]{2,1,0:T(4,128)(2,1)S(1)} %get-tuple-element.15.refs_0_, bf16[2,4,1024]{2,1,0:T(4,128)(2,1)S(1)} %get-tuple-element.16.refs_1_, ...), custom_call_target="tpu_custom_call" | custom-call | tf_op jit(solution)/shard_map/pallas_call | solution.py:598

commit v6 on v5

--- a/solution.py
+++ b/solution.py
@@ -57,9 +57,8 @@
 
 
 SENDS = 16
-FAR = (3, N - 3, 1, N - 1)
 FARTHEST_FIRST = (3, 5, 4, 2, 6, 1, 7)
-PHASES = 40
+PHASES = 38
 
 
 def kernel(
@@ -67,7 +66,7 @@
     out_ref, ing_ref, first_out, second_out, gg_ref,
     x_in, gain_ref, w1, w2, cot_ref, xp, u, u_o, cg, cg_o,
     s_a, r_a, s_sq, r_sq, s_c, r_c, hid, hid_o, q, q_o, p_own, slope, scl,
-    branch, r_fs, s_fz, r_fz, r_ff, r_f2, s_fx, r_fx,
+    branch, r_fs, s_fz, r_fz, s_fx, r_fx,
     big, r_gs, s_gz, r_gz, s_gx, r_gx,
     e_s, e_r, ee_own, ee_r1, ee_chip, ee_rz, ee_line, ee_rx, gg_own, gg_r1, gg_chip, gg_rz, gg_line, gg_rx,
     send_sems, recv_sems, local_sems,
@@ -298,111 +297,28 @@
 
     for phase in b_rest:
         phase.arrived()
-    hid_lo = Phase(lambda k: (hid, hid_o, lo_peer), 0, 1, sems)
-    hid_lo.start()
-    branch[...] = jnp.dot(
-        hid[...].reshape(256, HID), w2[...], preferred_element_type=F32
-    ).reshape(2, 128, FEAT)
     sib_rows = pl.ds(pl.multiple_of(64 - 64 * c, 64), 64)
-    f_sib = Phase(lambda k: (branch.at[:, sib_rows], r_fs, sib_peer), 0, 1, sems)
-    f_sib.start()
+    f_sibs = [
+        Phase(lambda k, h=h: (branch.at[h, sib_rows], r_fs.at[h], sib_peer), 0, 1, sems)
+        for h in range(2)
+    ]
+    for h in range(2):
+        branch[h] = jnp.dot(hid[h], w2[...], preferred_element_type=F32)
+        f_sibs[h].start()
 
     u_lo.arrived()
     u_sib = Phase(lambda k: (u_o.at[:, core_rows], u_o.at[:, core_rows], sib_peer), 0, 1, sems)
     u_sib.start()
 
-    f_sib.arrived()
-    for h in range(2):
-        both = branch[h, core_rows] + r_fs[h]
-        s_fz[h] = both.reshape(N, 8, FEAT).astype(BF16)
-
-    def f_near(k):
-        step = N - 1 if k % 2 else 1
-        if k < 2:
-            return s_fz.at[:, z_place(2 * step)], r_fz.at[k], z_peer(step)
-        return s_fz.at[k - 2, z_place(4)], r_ff.at[k - 2], z_peer(step)
-
-    f_one = Phase(f_near, 0, 2, sems, r_fz)
-    f_one.start()
-    f_four = Phase(lambda k: f_near(k + 2), 0, 2, sems, r_ff)
-    f_four.start()
-
-    g_sibs = [
-        Phase(lambda k, h=h: (big.at[h, sib_rows], r_gs.at[h], sib_peer), 0, 1, sems)
-        for h in range(2)
-    ]
-    g_zs = [
-        Phase(
-            lambda k, h=h: (s_gz.at[h, z_place(k)], r_gz.at[h, k], z_peer(k)),
-            1,
-            N,
-            sems,
-            r_gz.at[h, pl.ds(1, N - 1)],
-        )
-        for h in range(2)
-    ]
-    q_lo = [
-        Phase(lambda k, h=h: (q.at[h], q_o.at[h], lo_peer), 0, 1, sems)
-        for h in range(2)
-    ]
-    f_far = Phase(
-        lambda k: (s_fz.at[:, z_place(FAR[k])], r_f2.at[k], z_peer(FAR[k])), 0, 4, sems, r_f2
-    )
-
-    def pass_f():
-        f_one.arrived()
-        f_four.arrived()
-        for k, step in ((0, 1), (1, N - 1)):
-            to = z_place(step)
-            for h in range(2):
-                s_fz[h, to] = (s_fz[h, to].astype(F32) + r_fz[k, h].astype(F32)).astype(BF16)
-            to = z_place(3 * step)
-            s_fz[k, to] = (s_fz[k, to].astype(F32) + r_ff[k].astype(F32)).astype(BF16)
-        f_far.start()
-
-    ee_sib = Phase(lambda k: (ee_own, ee_r1, sib_peer), 0, 1, sems)
-    ee_z = Phase(lambda k: (ee_chip, ee_rz.at[k], z_peer(k)), 1, N, sems, ee_rz.at[pl.ds(1, N - 1)])
-    gain_part = jnp.zeros((1, FEAT), F32)
-    for h in range(2):
-        d_y[h].arrived()
-        for rows in (sib_rows, core_rows):
-            part = lax.dot_general(q[h, rows], w1[...], NT, preferred_element_type=F32)
-            big[h, rows] = part
-            if rows is sib_rows:
-                g_sibs[h].start()
-        if h == 0:
-            e_y.arrived()
-            e_sum = e_s[...]
-            for k in range(1, N):
-                e_sum = e_sum + e_r[k]
-            ee_own[...] = e_sum
-            ee_sib.start()
-        q_lo[h].start()
-        gain_part = gain_part + jnp.sum(
-            big[h] * xp[h * 128 : (h + 1) * 128, :], axis=0, keepdims=True
-        )
-        if h == 0:
-            pass_f()
-        else:
-            gg_own[...] = gain_part
-            gg_sib = Phase(lambda k: (gg_own, gg_r1, sib_peer), 0, 1, sems)
-            gg_sib.start()
-        g_sibs[h].arrived()
-        both = big[h, core_rows] + r_gs[h]
-        s_gz[h] = both.reshape(N, 8, FEAT).astype(BF16)
-        if h == 1:
-            gg_sib.arrived()
-            gg_chip[...] = gg_own[...] + gg_r1[...]
-            gg_z = Phase(
-                lambda k: (gg_chip, gg_rz.at[k], z_peer(k)), 1, N, sems, gg_rz.at[pl.ds(1, N - 1)]
-            )
-            gg_z.start()
-        g_zs[h].start()
-        if h == 0:
-            ee_sib.arrived()
-            ee_chip[...] = ee_own[...] + ee_r1[...]
-            ee_z.start()
-
+    f_sibs[0].arrived()
+    s_fx[...] = (branch[0, core_rows] + r_fs[0]).astype(BF16)
+    f_xh = Phase(lambda k: (s_fx, r_fx, xh_peer), 0, 1, sems)
+    f_xh.start()
+    hid_lo = Phase(lambda k: (hid, hid_o, lo_peer), 0, 1, sems)
+    hid_lo.start()
+    f_z = Phase(
+        lambda k: (s_fz.at[z_place(k)], r_fz.at[k], z_peer(k)), 1, N, sems, r_fz.at[pl.ds(1, N - 1)]
+    )
     cot_sibo = [
         Phase(lambda k, h=h: (cg_o.at[pieces(h)], cg_o.at[pieces(h)], sib_peer), 0, 1, sems)
         for h in range(2)
@@ -411,6 +327,70 @@
     cot_sibo[1].start()
     cot_lo0.arrived()
     cot_sibo[0].start()
+
+    g_sibs = [
+        Phase(lambda k, h=h: (big.at[h, sib_rows], r_gs.at[h], sib_peer), 0, 1, sems)
+        for h in range(2)
+    ]
+    g_xh = Phase(lambda k: (s_gx, r_gx, xh_peer), 0, 1, sems)
+    g_z = Phase(
+        lambda k: (s_gz.at[z_place(k)], r_gz.at[k], z_peer(k)), 1, N, sems, r_gz.at[pl.ds(1, N - 1)]
+    )
+    q_lo = [
+        Phase(lambda k, h=h: (q.at[h], q_o.at[h], lo_peer), 0, 1, sems)
+        for h in range(2)
+    ]
+    ee_sib = Phase(lambda k: (ee_own, ee_r1, sib_peer), 0, 1, sems)
+    ee_z = Phase(lambda k: (ee_chip, ee_rz.at[k], z_peer(k)), 1, N, sems, ee_rz.at[pl.ds(1, N - 1)])
+
+    def normed_part(h):
+        d_y[h].arrived()
+        for rows in (sib_rows, core_rows):
+            big[h, rows] = lax.dot_general(
+                q[h, rows], w1[...], NT, preferred_element_type=F32
+            )
+            if rows is sib_rows:
+                g_sibs[h].start()
+
+    def gain_part(h):
+        return jnp.sum(big[h] * xp[h * 128 : (h + 1) * 128, :], axis=0, keepdims=True)
+
+    normed_part(0)
+    e_y.arrived()
+    e_sum = e_s[...]
+    for k in range(1, N):
+        e_sum = e_sum + e_r[k]
+    ee_own[...] = e_sum
+    ee_sib.start()
+    g_sibs[0].arrived()
+    s_gx[...] = (big[0, core_rows] + r_gs[0]).astype(BF16)
+    g_xh.start()
+    ee_sib.arrived()
+    ee_chip[...] = ee_own[...] + ee_r1[...]
+    ee_z.start()
+    q_lo[0].start()
+    gain_first = gain_part(0)
+
+    normed_part(1)
+    gg_own[...] = gain_first + gain_part(1)
+    gg_sib = Phase(lambda k: (gg_own, gg_r1, sib_peer), 0, 1, sems)
+    gg_sib.start()
+    f_sibs[1].arrived()
+    f_xh.arrived()
+    f_sum = branch[1, core_rows] + r_fs[1] + r_fx[...].astype(F32)
+    s_fz[...] = f_sum.reshape(N, 8, FEAT).astype(BF16)
+    f_z.start()
+    gg_sib.arrived()
+    gg_chip[...] = gg_own[...] + gg_r1[...]
+    gg_z = Phase(lambda k: (gg_chip, gg_rz.at[k], z_peer(k)), 1, N, sems, gg_rz.at[pl.ds(1, N - 1)])
+    gg_z.start()
+    g_sibs[1].arrived()
+    g_xh.arrived()
+    g_sum = big[1, core_rows] + r_gs[1] + r_gx[...].astype(F32)
+    s_gz[...] = g_sum.reshape(N, 8, FEAT).astype(BF16)
+    g_z.start()
+    q_lo[1].start()
+
     hid_lo.arrived()
     for h in range(2):
         cot_sibo[h].arrived()
@@ -424,16 +404,10 @@
         hid_all, cot_all, TN, preferred_element_type=F32
     ).astype(BF16)
 
-    def z_total(sent, received, h):
-        total = sent[h, z].astype(F32)
+    def z_total(sent, received):
+        total = sent[z].astype(F32)
         for k in range(1, N):
-            total = total + received(k)
-        return total
-
-    def f_total(h):
-        total = s_fz[h, z].astype(F32)
-        for k in range(4):
-            total = total + r_f2[k, h].astype(F32)
+            total = total + received[k].astype(F32)
         return total
 
     ee_z.arrived()
@@ -443,17 +417,6 @@
     ee_line[...] = ee_total
     ee_xh = Phase(lambda k: (ee_line, ee_rx, xh_peer), 0, 1, sems)
     ee_xh.start()
-
-    f_far.arrived()
-    s_fx[...] = f_total(0)
-    f_xh = Phase(lambda k: (s_fx, r_fx, xh_peer), 0, 1, sems)
-    f_xh.start()
-    own_branch = f_total(1)
-
-    g_zs[0].arrived()
-    s_gx[...] = z_total(s_gz, lambda k: r_gz[0, k].astype(F32), 0)
-    g_xh = Phase(lambda k: (s_gx, r_gx, xh_peer), 0, 1, sems)
-    g_xh.start()
 
     gg_z.arrived()
     gg_total = gg_chip[...]
@@ -474,15 +437,13 @@
     first_out[...] = lax.dot_general(u_all, q_all, TN, preferred_element_type=F32).astype(BF16)
 
     x_own = xp[pl.ds(pl.multiple_of(mine * 8, 8), 8), :]
-    f_xh.arrived()
-    outputs = x_own + own_branch + r_fx[...]
+    f_z.arrived()
+    outputs = x_own + z_total(s_fz, r_fz)
     out_ref[0] = outputs[0:4].astype(BF16)
     out_ref[1] = outputs[4:8].astype(BF16)
 
-    g_zs[1].arrived()
-    normed_grad = z_total(s_gz, lambda k: r_gz[1, k].astype(F32), 1)
-    g_xh.arrived()
-    normed_grad = normed_grad + r_gx[...]
+    g_z.arrived()
+    normed_grad = z_total(s_gz, r_gz)
     ee_xh.arrived()
     inner_row = ee_line[:, 128:256] + ee_rx[:, 0:128]
     own_lane = lax.broadcasted_iota(jnp.int32, (8, 128), 1)
@@ -498,6 +459,7 @@
     gg_x.arrived()
     gg_ref[...] = (gg_line[...] + gg_rx[0]) + (gg_rx[1] + gg_rx[2])
 
+    assert sems["used"] == PHASES
     for phase in sems["phases"][-SENDS:]:
         phase.sent()
 
@@ -541,18 +503,16 @@
         ((2, 16, 128), F32),
         ((2, 128, FEAT), F32),
         ((2, 64, FEAT), F32),
-        ((2, N, 8, FEAT), BF16),
-        ((2, 2, 8, FEAT), BF16),
-        ((2, 8, FEAT), BF16),
-        ((4, 2, 8, FEAT), BF16),
-        ((8, FEAT), F32),
-        ((8, FEAT), F32),
+        ((N, 8, FEAT), BF16),
+        ((N, 8, FEAT), BF16),
+        ((64, FEAT), BF16),
+        ((64, FEAT), BF16),
         ((2, 128, FEAT), F32),
         ((2, 64, FEAT), F32),
-        ((2, N, 8, FEAT), BF16),
-        ((2, N, 8, FEAT), BF16),
-        ((8, FEAT), F32),
-        ((8, FEAT), F32),
+        ((N, 8, FEAT), BF16),
+        ((N, 8, FEAT), BF16),
+        ((64, FEAT), BF16),
+        ((64, FEAT), BF16),
         ((1, 256), F32),
         ((N, 1, 256), F32),
         ((1, 256), F32),

time: 56.8 us -> 58.9 us (1.037); the launches traced: 55.9 us -> 58.7 us
  Pallas kernels: 55.2 us -> 58.1 us
    pallas_call x1, Pallas kernels: 53.9 us -> 56.7 us  [per_device(): pl.pallas_call(kernel, out_shape=results, in_specs=[hbm] * 5, out_specs=(...]
where the time goes in v6:
time: 58.9 us; the launch traced here: 58.7 us
  Pallas kernels  58.1 us (99%)
  between operations  0.64 us (1%)
    pallas_call x1, Pallas kernels, per_device(): pl.pallas_call(kernel, out_shape=results, in_specs=[hbm] * 5, out_specs=(...  56.7 us
    pallas_call x1, Pallas kernels, per_device(): pl.pallas_call(save, out_shape=results, in_specs=[vmem] * 5, out_specs=(a...  1.38 us

profile of v6, /device:TPU:1, one launch (start us, length us, event | category | flops | bytes accessed | tf_op | source)
XLA Modules:
  0.0 58.7 jit_solution(1030145234069042966)
XLA Ops:
  0.6 56.7 %shard_map.92 = (bf16[2,4,1024]{2,1,0:T(4,128)(2,1)S(1)}, bf16[2,4,1024]{2,1,0:T(4,128)(2,1)S(1)}, bf16[1024,512]{1,0:T(8,128)(2,1)S(1)}, bf16[512,1024]{1,0:T(8,128)(2,1)S(1)}, f32[1,1024]{1,0:T(1,128)S(1)}) custom-call(bf16[2,128,1024]{2,1,0:T(8,128)(2,1)} %x_hbm.1, f32[1,1024]{1,0:T(1,128)} %bitcast.2, bf16[1024,512]{1,0:T(8,128)(2,1)} %w1_hbm.1, ...), custom_call_target="tpu_custom_call" | custom-call | tf_op jit(solution)/shard_map/pallas_call | solution.py:538
  57.3 1.4 %shard_map.93 = (bf16[2,4,1024]{2,1,0:T(4,128)(2,1)}, bf16[2,4,1024]{2,1,0:T(4,128)(2,1)}, bf16[1024,512]{1,0:T(8,128)(2,1)}, bf16[512,1024]{1,0:T(8,128)(2,1)}, f32[1,1024]{1,0:T(1,128)}) custom-call(bf16[2,4,1024]{2,1,0:T(4,128)(2,1)S(1)} %get-tuple-element.15.refs_0_, bf16[2,4,1024]{2,1,0:T(4,128)(2,1)S(1)} %get-tuple-element.16.refs_1_, ...), custom_call_target="tpu_custom_call" | custom-call | tf_op jit(solution)/shard_map/pallas_call | solution.py:558

commit v7 on v5

--- a/solution.py
+++ b/solution.py
@@ -381,9 +381,8 @@
         gain_part = gain_part + jnp.sum(
             big[h] * xp[h * 128 : (h + 1) * 128, :], axis=0, keepdims=True
         )
-        if h == 0:
+        if h == 1:
             pass_f()
-        else:
             gg_own[...] = gain_part
             gg_sib = Phase(lambda k: (gg_own, gg_r1, sib_peer), 0, 1, sems)
             gg_sib.start()

time: 56.8 us -> 55.7 us (0.981)
  Pallas kernels: 55.2 us -> 54 us
    pallas_call x1, Pallas kernels: 53.9 us -> 52.6 us  [per_device(): pl.pallas_call(kernel, out_shape=results, in_specs=[hbm] * 5, out_specs=(...]
where the time goes in v7:
time: 55.7 us; the launch traced here: 54.6 us
  Pallas kernels  54 us (97%)
  between operations  0.64 us (1%)
    pallas_call x1, Pallas kernels, per_device(): pl.pallas_call(kernel, out_shape=results, in_specs=[hbm] * 5, out_specs=(...  52.6 us
    pallas_call x1, Pallas kernels, per_device(): pl.pallas_call(save, out_shape=results, in_specs=[vmem] * 5, out_specs=(a...  1.38 us

profile of v7, /device:TPU:1, one launch (start us, length us, event | category | flops | bytes accessed | tf_op | source)
XLA Modules:
  0.0 54.6 jit_solution(7174340711925578389)
XLA Ops:
  0.6 52.6 %shard_map.92 = (bf16[2,4,1024]{2,1,0:T(4,128)(2,1)S(1)}, bf16[2,4,1024]{2,1,0:T(4,128)(2,1)S(1)}, bf16[1024,512]{1,0:T(8,128)(2,1)S(1)}, bf16[512,1024]{1,0:T(8,128)(2,1)S(1)}, f32[1,1024]{1,0:T(1,128)S(1)}) custom-call(bf16[2,128,1024]{2,1,0:T(8,128)(2,1)} %x_hbm.1, f32[1,1024]{1,0:T(1,128)} %bitcast.2, bf16[1024,512]{1,0:T(8,128)(2,1)} %w1_hbm.1, ...), custom_call_target="tpu_custom_call" | custom-call | tf_op jit(solution)/shard_map/pallas_call | solution.py:577
  53.3 1.4 %shard_map.93 = (bf16[2,4,1024]{2,1,0:T(4,128)(2,1)}, bf16[2,4,1024]{2,1,0:T(4,128)(2,1)}, bf16[1024,512]{1,0:T(8,128)(2,1)}, bf16[512,1024]{1,0:T(8,128)(2,1)}, f32[1,1024]{1,0:T(1,128)}) custom-call(bf16[2,4,1024]{2,1,0:T(4,128)(2,1)S(1)} %get-tuple-element.15.refs_0_, bf16[2,4,1024]{2,1,0:T(4,128)(2,1)S(1)} %get-tuple-element.16.refs_1_, ...), custom_call_target="tpu_custom_call" | custom-call | tf_op jit(solution)/shard_map/pallas_call | solution.py:597
